TPU v7x, 256 devices: a whole 4x4x8 slice. The times are simulated.
256 devices in a mesh: dp: 4 (over z_hi, core), chan: 4 (over x), space: 16 (over z_lo, y).
Axes of the slice: x: 4, y: 4, z: 8 (z_hi: 2, z_lo: 4; z = z_hi * 4 + z_lo), core: 2. Of those that a mesh axis runs over, the one named last changes fastest.
Arguments:
- section_input: bfloat16 [4, 2, 128, 128, 512], P('dp', None, 'space', None, 'chan'), may hold values from -6 to 6
- middle: bfloat16 [4, 2, 128, 128, 512], P('dp', None, 'space', None, 'chan'), may hold values from -6 to 6
- out_grad: bfloat16 [4, 2, 128, 128, 512], P('dp', None, 'space', None, 'chan'), may hold values from -6 to 6
- kernels: bfloat16 [2, 3, 3, 512, 512], P(None, None, None, None, 'chan'), may hold values from -0.09375 to 0.09375
- master: float32 [2, 3, 3, 512, 512], P(None, None, None, ('dp', 'space'), 'chan'), may hold values from -0.09375 to 0.09375
- moment: float32 [2, 3, 3, 512, 512], P(None, None, None, ('dp', 'space'), 'chan'), may hold values from -600 to 600
- second: float32 [2, 3, 3, 512, 512], P(None, None, None, ('dp', 'space'), 'chan'), may hold values from 1000 to 100000
Outputs:
- input_grad: bfloat16 [4, 2, 128, 128, 512], P('dp', None, 'space', None, 'chan')
- new_kernels: bfloat16 [2, 3, 3, 512, 512], P(None, None, None, None, 'chan')
- new_master: float32 [2, 3, 3, 512, 512], P(None, None, None, ('dp', 'space'), 'chan')
- new_moment: float32 [2, 3, 3, 512, 512], P(None, None, None, ('dp', 'space'), 'chan')
- new_second: float32 [2, 3, 3, 512, 512], P(None, None, None, ('dp', 'space'), 'chan')
All inputs are finite; a program needn't handle non-finite values.
Results may differ from a plain program's by a relative error of at most 0.0015.
The roundings to bfloat16 on the way count: a program that leaves them out, or rounds other values in their place, can miss the bound.
Values may be sent and summed in bfloat16 or wider, within the bound.
A program may use at most 128 MiB of HBM per device.

v0:
```python
import jax
import jax.numpy as jnp
from jax import lax
from jax.sharding import PartitionSpec as P


def with_halo(x, sides, width):
    for axis, dim in sides:
        size, length = (lax.axis_size(axis), x.shape[dim])
        up = [(i, (i + 1) % size) for i in range(size - 1)]
        down = [(j, i) for i, j in up]
        last = lax.slice_in_dim(x, length - width, length, axis=dim)
        initial = lax.slice_in_dim(x, 0, width, axis=dim)
        before = lax.ppermute(last, axis, up)
        after = lax.ppermute(initial, axis, down)
        x = jnp.concatenate([before, x, after], axis=dim)
    return x


def dsilu(value):
    sig = jax.nn.sigmoid(value)
    return sig * (1.0 + value * (1.0 - sig))


def tap_views(padded, rows, cols):
    return [
        padded[:, :, 2 - row_tap : 2 - row_tap + rows, 2 - col_tap : 2 - col_tap + cols, :].reshape(
            -1, padded.shape[4]
        )
        for row_tap in range(3)
        for col_tap in range(3)
    ]


def conv_back(act, grad, weight):
    rows = grad.shape[2]
    cols = grad.shape[3]
    rims = with_halo(grad, (("space", 2),), 1)
    local_out = grad.shape[4]
    padded = jnp.pad(rims, ((0, 0), (0, 0), (0, 0), (1, 1), (0, 0)))
    views = tap_views(padded, rows, cols)
    piece = lax.all_gather(act, "chan", axis=4, tiled=True)
    flat = piece.reshape(-1, piece.shape[4])
    blocks = [
        lax.dot_general(flat, view, (((0,), (0,)), ((), ())), preferred_element_type=jnp.float32)
        for view in views
    ]
    kernel_grad = jnp.stack(blocks).reshape(3, 3, flat.shape[1], local_out)
    full_in = weight.shape[2]
    partial_value = jnp.zeros((views[0].shape[0], full_in), jnp.float32)
    for tap in range(9):
        partial_value = partial_value + lax.dot_general(
            views[tap],
            weight[tap // 3, tap % 3],
            (((1,), (1,)), ((), ())),
            preferred_element_type=jnp.float32,
        )
    partial_value = partial_value.reshape(grad.shape[:4] + (full_in,))
    back = lax.psum_scatter(partial_value, "chan", scatter_dimension=4, tiled=True)
    return (kernel_grad, back)


def on_device(section_input, middle, out_grad, kernels, master, moment, second):
    mid_f = middle.astype(jnp.float32)
    in_f = section_input.astype(jnp.float32)
    act2 = jax.nn.silu(mid_f).astype(jnp.bfloat16)
    grad2, back2 = conv_back(act2, out_grad, kernels[1])
    mid_grad = (back2 * dsilu(mid_f)).astype(jnp.bfloat16)
    act1 = jax.nn.silu(in_f).astype(jnp.bfloat16)
    grad1, back1 = conv_back(act1, mid_grad, kernels[0])
    input_grad = (out_grad.astype(jnp.float32) + back1 * dsilu(in_f)).astype(jnp.bfloat16)
    grads = jnp.stack([grad1, grad2])
    owned = master.shape[3]
    totals = lax.psum(grads, ("dp", "space"))
    shares = lax.dynamic_slice_in_dim(totals, lax.axis_index(("dp", "space")) * owned, owned, 3)
    new_moment = 0.9 * moment + 0.1 * shares
    new_second = 0.999 * second + 0.001 * shares * shares
    corrected = new_moment / (1.0 - 0.9**10)
    scale_term = jnp.sqrt(new_second / (1.0 - 0.999**10)) + 1e-08
    new_master = master - 0.01 * corrected / scale_term
    new_kernels = lax.all_gather(
        new_master.astype(jnp.bfloat16), ("dp", "space"), axis=3, tiled=True
    )
    return (input_grad, new_kernels, new_master, new_moment, new_second)


def solution(mesh):
    placed = (
        P("dp", None, "space", None, "chan"),
        P("dp", None, "space", None, "chan"),
        P("dp", None, "space", None, "chan"),
        P(None, None, None, None, "chan"),
        P(None, None, None, ("dp", "space"), "chan"),
        P(None, None, None, ("dp", "space"), "chan"),
        P(None, None, None, ("dp", "space"), "chan"),
    )
    return jax.shard_map(
        on_device,
        mesh=mesh,
        in_specs=placed,
        out_specs=(
            P("dp", None, "space", None, "chan"),
            P(None, None, None, None, "chan"),
            P(None, None, None, ("dp", "space"), "chan"),
            P(None, None, None, ("dp", "space"), "chan"),
            P(None, None, None, ("dp", "space"), "chan"),
        ),
        check_vma=False,
    )
```

profile of v0, /device:TPU:1, one launch (start us, length us, event | category | flops | bytes accessed | tf_op | source)
XLA Modules:
  0.0 640.3 jit_solution(10813237290408105905)
XLA Ops:
  8.1 4.0 collective-permute-start
  13.6 2.8 slice_bitcast_fusion
  19.6 2.6 fusion.195
  22.2 2.7 fusion.197
  24.9 2.7 fusion.198
  27.6 2.7 fusion.200
  30.4 2.7 fusion.199
  33.1 11.3 %add_add_fusion.1 = f32[2048,512]{1,0:T(8,128)} fusion(f32[2048,512]{1,0:T(8,128)S(1)} %fusion.193, f32[2048,512]{1,0:T(8,128)S(1)} %fusion.194, f32[2048,512]{1,0:T(8,128)} %fusion.195, f32[2048,512]{1,0:T(8,128)S(1)} %fusion.196, f32[2048,512]{1,0:T(8,128)} %fusion.197, f32[2048,512]{1,0:T(8,128)} %fusion.198, f32[2048,512]{1,0:T(8,128)} %fusion.200, ...), kind=kOutput, calls=%fused_computation.2 | convolution fusion | flops 276824064 | bytes 38404096 | tf_op jit(solution)/shard_map/dot_general | solution.py:52
  44.5 54.9 %reduce-scatter.3.cloned.1.call-done = f32[1,2,8,128,128]{4,3,2,1,0:T(8,128)} async-done(((f32[1,2,8,128,512]{4,3,2,1,0:T(8,128)}), f32[1,2,8,128,128]{4,3,2,1,0:T(8,128)}) %reduce-scatter.3.cloned.1.call-update) | async-done | bytes 1048592 | tf_op jit(solution)/shard_map/reduce_scatter | solution.py:59
  99.4 2.5 fusion.152
  101.9 3.1 collective-permute-start.2
  105.0 1.5 collective-permute-start.3
  106.5 1.7 fusion.188
  108.2 1.8 collective-permute-done.3
  113.3 2.7 fusion.187
  115.9 2.7 fusion.189
  118.6 2.7 fusion.190
  121.4 2.6 fusion.192
  124.0 2.7 fusion.185
  126.7 11.4 %add_add_fusion = f32[2048,512]{1,0:T(8,128)} fusion(f32[2048,512]{1,0:T(8,128)} %fusion.185, f32[2048,512]{1,0:T(8,128)S(1)} %fusion.186, f32[2048,512]{1,0:T(8,128)} %fusion.187, f32[2048,512]{1,0:T(8,128)S(1)} %fusion.188, f32[2048,512]{1,0:T(8,128)} %fusion.189, f32[2048,512]{1,0:T(8,128)} %fusion.190, f32[2048,512]{1,0:T(8,128)} %fusion.192, ...), kind=kOutput, calls=%fused_computation.1 | convolution fusion | flops 276824064 | bytes 38404096 | tf_op jit(solution)/shard_map/dot_general | solution.py:52
  138.9 50.8 %reduce-scatter.5.cloned.1.call-done = f32[1,2,8,128,128]{4,3,2,1,0:T(8,128)} async-done(((f32[1,2,8,128,512]{4,3,2,1,0:T(8,128)}), f32[1,2,8,128,128]{4,3,2,1,0:T(8,128)}) %reduce-scatter.5.cloned.1.call-update) | async-done | bytes 1048592 | tf_op jit(solution)/shard_map/reduce_scatter | solution.py:59
  189.7 2.9 fusion.161
  192.9 34.5 %all-gather.6.cloned.1.call-done = bf16[1,2,8,128,512]{4,3,2,1,0:T(8,128)(2,1)} async-done(((bf16[1,2,8,128,128]{4,3,2,1,0:T(8,128)(2,1)}), bf16[1,2,8,128,512]{4,3,2,1,0:T(8,128)(2,1)}) %all-gather.6.cloned.1.call-update) | async-done | bytes 2097168 | tf_op jit(solution)/shard_map/all_gather | solution.py:42
  227.4 3.2 fusion.94
  230.6 1.4 fusion.100
  242.2 25.0 %all-gather.4.cloned.1.call-done = bf16[1,2,8,128,512]{4,3,2,1,0:T(8,128)(2,1)} async-done(((bf16[1,2,8,128,128]{4,3,2,1,0:T(8,128)(2,1)}), bf16[1,2,8,128,512]{4,3,2,1,0:T(8,128)(2,1)}) %all-gather.4.cloned.1.call-update) | async-done | bytes 2097168 | tf_op jit(solution)/shard_map/all_gather | solution.py:42
  267.2 2.5 fusion.40
  275.7 4.3 pad_maximum_fusion
  280.1 196.5 %all-reduce.4.cloned.1.call-done = f32[2,3,3,512,128]{4,3,2,1,0:T(8,128)} async-done(((f32[2,3,3,512,128]{4,3,2,1,0:T(8,128)}), f32[2,3,3,512,128]{4,3,2,1,0:T(8,128)}) %all-reduce.4.cloned.1.call-update) | async-done | bytes 4718608 | tf_op jit(solution)/shard_map/psum | solution.py:74
  476.6 1.6 fusion.214
  478.2 152.0 %all-gather.8.cloned.1.call-done = bf16[2,3,3,512,128]{4,3,2,1,0:T(8,128)(2,1)} async-done(((bf16[2,3,3,8,128]{4,3,2,1,0:T(8,128)(2,1)}), bf16[2,3,3,512,128]{4,3,2,1,0:T(8,128)(2,1)}) %all-gather.8.cloned.1.call-update) | async-done | bytes 2359312 | tf_op jit(solution)/shard_map/all_gather | solution.py:81
  630.2 3.3 copy.84
  (68 shorter events, 26.1 us)
Async XLA Ops:
  7.2 92.2 %reduce-scatter.3.cloned.1.call-start = ((), (), s32[]{:S(2)}) async-start(), calls=%async_computation.2 | async-start | bytes 5242880 | tf_op jit(solution)/shard_map/reduce_scatter | solution.py:59
  8.1 9.0 %collective-permute-start = (bf16[1,2,1,128,128]{4,3,2,1,0:T(8,128)(2,1)S(1)}, bf16[1,2,1,128,128]{4,3,2,1,0:T(8,128)(2,1)S(1)}, u32[]{:S(2)}, u32[]{:S(2)}) collective-permute-start(bf16[1,2,1,128,128]{4,3,2,1,0:T(8,128)(2,1)S(1)} %get-tuple-element.33), channel_id=1, source_target_pairs={{0,1},{1,2},{2,3},{3,4},{4,5},{5,6},{6,7},{7,8},{8,9},{9,10},{10,1... | collective-permute-start | bytes 196616 | tf_op jit(solution)/shard_map/ppermute | solution.py:14
  12.1 4.3 copy-start.2
  12.2 5.1 collective-permute-start.1
  30.4 2.7 copy-start.4
  44.4 55.0 %copy-start.8 = (bf16[1,2,8,128,128]{4,3,2,1,0:T(8,128)(2,1)S(1)}, bf16[1,2,8,128,128]{4,3,2,1,0:T(8,128)(2,1)}, u32[]{:S(2)}) copy-start(bf16[1,2,8,128,128]{4,3,2,1,0:T(8,128)(2,1)} %param.8) | copy-start | bytes 1572868
  44.4 145.3 %reduce-scatter.5.cloned.1.call-start = ((), (), s32[]{:S(2)}) async-start(), calls=%async_computation.3 | async-start | bytes 5242880 | tf_op jit(solution)/shard_map/reduce_scatter | solution.py:59
  101.9 6.3 collective-permute-start.2
  105.0 5.0 collective-permute-start.3
  106.5 4.4 copy-start.3
  110.1 0.8 copy-start.6
  138.1 89.3 %all-gather.6.cloned.1.call-start = ((), (), s32[]{:S(2)}) async-start(), calls=%async_computation.5 | async-start | bytes 2621440 | tf_op jit(solution)/shard_map/all_gather | solution.py:42
  138.8 128.3 %all-gather.4.cloned.1.call-start = ((), (), s32[]{:S(2)}) async-start(), calls=%async_computation.4 | async-start | bytes 2621440 | tf_op jit(solution)/shard_map/all_gather | solution.py:42
  192.7 283.9 %all-reduce.4.cloned.1.call-start = ((), (), s32[]{:S(2)}) async-start(), calls=%async_computation.6 | async-start | bytes 9437184 | tf_op jit(solution)/shard_map/psum | solution.py:74
  227.4 3.2 copy-start.1
  227.4 3.2 copy-start.5
  242.2 27.5 %copy-start.7 = (bf16[1,2,8,128,128]{4,3,2,1,0:T(8,128)(2,1)S(1)}, bf16[1,2,8,128,128]{4,3,2,1,0:T(8,128)(2,1)}, u32[]{:S(2)}) copy-start(bf16[1,2,8,128,128]{4,3,2,1,0:T(8,128)(2,1)} %copy-done.6) | copy-start | bytes 1572868
  267.2 2.5 copy-start
  280.0 196.6 %copy-start.9 = (f32[2,3,3,8,128]{4,3,2,1,0:T(8,128)S(1)}, f32[2,3,3,8,128]{4,3,2,1,0:T(8,128)}, u32[]{:S(2)}) copy-start(f32[2,3,3,8,128]{4,3,2,1,0:T(8,128)} %param.11) | copy-start | bytes 221188
  280.0 196.6 %copy-start.10 = (f32[2,3,3,8,128]{4,3,2,1,0:T(8,128)S(1)}, f32[2,3,3,8,128]{4,3,2,1,0:T(8,128)}, u32[]{:S(2)}) copy-start(f32[2,3,3,8,128]{4,3,2,1,0:T(8,128)} %param.12) | copy-start | bytes 221188
  280.0 196.6 %copy-start.11 = (f32[2,3,3,8,128]{4,3,2,1,0:T(8,128)S(1)}, f32[2,3,3,8,128]{4,3,2,1,0:T(8,128)}, u32[]{:S(2)}) copy-start(f32[2,3,3,8,128]{4,3,2,1,0:T(8,128)} %param.13) | copy-start | bytes 221188
  280.0 350.2 %all-gather.8.cloned.1.call-start = ((), (), s32[]{:S(2)}) async-start(), calls=%async_computation.7 | async-start | bytes 2396160 | tf_op jit(solution)/shard_map/all_gather | solution.py:81
Sparse Core Ops, SparseCore 0:
  44.5 54.8 reduce-scatter.2
  138.2 51.4 reduce-scatter.4
  191.5 35.8 all-gather.5
  229.1 38.0 all-gather.3
  280.2 196.3 all-reduce.3
  478.9 151.2 all-gather.7
where the time goes:
time: 641 us; the launch traced here: 640 us
  waiting for transfers between devices  516 us (80%)
  matrix products  78 us (12%)
  between operations  14.4 us (2%)
  other arithmetic  11.8 us (2%)
  starting transfers between devices  10.5 us (2%)
  local copies, waits for them, and re-layouts  9.17 us (1%)
    psum x1, waiting for transfers between devices, on_device(): totals = lax.psum(grads, ('dp', 'space'))  197 us
    all_gather x1, waiting for transfers between devices, on_device(): lax.all_gather(new_master.astype(jnp.bfloat16), ('dp', 'space'), axis=3,...  152 us
    reduce_scatter x2, waiting for transfers between devices, conv_back(): lax.psum_scatter(partial_value, 'chan', scatter_dimension=4, tiled=True)  106 us
    all_gather x2, waiting for transfers between devices, conv_back(): piece = lax.all_gather(act, 'chan', axis=4, tiled=True)  59.4 us
    dot_general x18, matrix products, conv_back(): lax.dot_general(views[tap], weight[tap // 3, tap % 3], (((1,), (1,)), (()...  54.8 us
    dot_general x18, matrix products, conv_back(): lax.dot_general(flat, view, (((0,), (0,)), ((), ())), preferred_element_t...  23.3 us
  transfers between devices with their start and end apart: 10, of which 8 were waited for; matrix products, arithmetic and copies ran while one was open for 4% of the time, Pallas kernels for 0%

commit v1 on v0

v1 whole, which is shorter than its diff:
```python
import jax
import jax.numpy as jnp
from jax import lax
from jax.experimental import pallas as pl
from jax.experimental.pallas import tpu as pltpu
from jax.sharding import PartitionSpec as P

BF = jnp.bfloat16
F32 = jnp.float32
MESH = pl.DeviceIdType.MESH
PX = 1024
SLAB = 80
VMEM_LIMIT = 56 * 1024 * 1024


def sigmoid(v):
    return 1.0 / (1.0 + jnp.exp(-v))


def dsilu(v):
    sig = sigmoid(v)
    return sig * (1.0 + v * (1.0 - sig))


def nt_dot(a, b):
    return lax.dot_general(a, b, (((1,), (1,)), ((), ())), preferred_element_type=F32)


class Sems:
    def __init__(self, ref):
        self.ref = ref
        self.used = 0

    def take(self, count=1):
        base = self.used
        self.used += count
        return base


def kernel(
    x_in, mid_in, og_in, kern, master, moment, second,
    ig_out, slab_out, master_out, moment_out, second_out,
    xpad, midpad, gog, gmg, w, actt, red, back, halo_in, halo_out, core_in,
    ysend, yrecv, zsend, zrecv, perm_src, perm_dst, adam_in, adam_out, slabs, ig_buf, sems,
):
    chan = lax.axis_index("chan")
    dp = lax.axis_index("dp")
    space = lax.axis_index("space")
    z_hi, core = dp // 2, dp % 2
    z_lo, y = space // 4, space % 4
    z = z_hi * 4 + z_lo
    pool = Sems(sems)
    sends = []

    def at_chan(p):
        return {"chan": (chan + p) % 4}

    def at_y(p):
        return {"space": z_lo * 4 + (y + p) % 4}

    def at_z(p):
        other = (z + p) % 8
        return {"dp": (other // 4) * 2 + core, "space": (other % 4) * 4 + y}

    sibling = {"dp": z_hi * 2 + (1 - core)}
    mirror = {"dp": chan, "chan": dp}
    has_prev = space > 0
    has_next = space < 15
    crosses = chan != dp

    def send(src, dst, target, recv_sem, when=None):
        copy = pltpu.make_async_remote_copy(
            src_ref=src, dst_ref=dst, send_sem=sems.at[pool.take()], recv_sem=sems.at[recv_sem],
            device_id=target, device_id_type=MESH,
        )
        if when is None:
            copy.start()
        else:
            pl.when(when)(copy.start)
        sends.append((copy, when))

    def wait_in(dst, sem):
        pltpu.make_async_copy(dst, dst, sems.at[sem]).wait()

    def load(src, dst):
        copy = pltpu.make_async_copy(src, dst, sems.at[pool.take()])
        copy.start()
        return copy

    inside = pl.ds(128, PX)
    load_mid = load(mid_in, midpad.at[:, inside, :])
    load_x = load(x_in, xpad.at[:, inside, :])
    load_og = load(og_in, gog.at[:, inside, pl.ds(0, 128)])
    my_rows = pl.ds(core * 64 + y * 16, 16)
    load_w = [
        load(kern.at[l, :, pl.ds(chan * 128 + core * 64 + y * 16, 16), :], w.at[l, :, my_rows, pl.ds(0, 128)])
        for l in range(2)
    ]
    load_adam = [load(ref, adam_in.at[k]) for k, ref in enumerate((master, moment, second))]

    barrier = pltpu.get_barrier_semaphore()

    def greet(target):
        pl.semaphore_signal(barrier, inc=1, device_id=target, device_id_type=MESH)

    for p in range(1, 4):
        greet(at_chan(p))
        greet(at_y(p))
    for p in range(1, 8):
        greet(at_z(p))
    greet(sibling)
    prev, nxt = {"space": space - 1}, {"space": space + 1}
    pl.when(has_prev)(lambda: greet(prev))
    pl.when(has_next)(lambda: greet(nxt))
    pl.when(crosses)(lambda: greet(mirror))

    zero_row = jnp.zeros((128, 512), BF)
    for g in (gog, gmg):
        for f in range(2):
            g[f, pl.ds(0, 128), :] = zero_row
            g[f, pl.ds(128 + PX, 128), :] = zero_row

    @pl.when(space == 0)
    def _():
        for pad in (midpad, xpad):
            pad[:, pl.ds(0, 128), :] = jnp.zeros((2, 128, 128), BF)

    @pl.when(space == 15)
    def _():
        for pad in (midpad, xpad):
            pad[:, pl.ds(128 + PX, 128), :] = jnp.zeros((2, 128, 128), BF)

    expected = 14 + has_prev.astype(jnp.int32) + has_next.astype(jnp.int32) + crosses.astype(jnp.int32)
    pl.semaphore_wait(barrier, expected)

    gathers = {}

    def half(f, h):
        return (f, pl.ds(128 + 512 * h, 512))

    def gather_own(name, g, src, f):
        sem = gathers.setdefault(name, {})
        for k in ("left", "right", "far"):
            for h in range(2):
                sem[k, f, h] = pool.take()
        for step in range(2):
            h = step
            send(src(f, h), g.at[(*half(f, h), pl.ds(128, 128))], at_chan(1), sem["left", f, h])
            h = 1 - step
            send(src(f, h), g.at[(*half(f, h), pl.ds(384, 128))], at_chan(3), sem["right", f, h])

    def gather_forward(name, g, f):
        sem = gathers[name]
        here = g.at[(*half(f, 0), pl.ds(128, 128))]
        wait_in(here, sem["left", f, 0])
        send(here, g.at[(*half(f, 0), pl.ds(256, 128))], at_chan(1), sem["far", f, 0])
        here = g.at[(*half(f, 1), pl.ds(384, 128))]
        wait_in(here, sem["right", f, 1])
        send(here, g.at[(*half(f, 1), pl.ds(256, 128))], at_chan(3), sem["far", f, 1])

    def gather_wait(name, g, f):
        sem = gathers[name]
        wait_in(g.at[(*half(f, 1), pl.ds(128, 128))], sem["left", f, 1])
        wait_in(g.at[(*half(f, 0), pl.ds(384, 128))], sem["right", f, 0])
        for h in range(2):
            wait_in(g.at[(*half(f, h), pl.ds(256, 128))], sem["far", f, h])

    w_sem = {}

    def weights_chan(l):
        for p in range(1, 4):
            w_sem["x", l, p] = pool.take()
            their = (chan + p) % 4
            send(
                kern.at[l, :, pl.ds(their * 128 + core * 64 + y * 16, 16), :],
                w.at[l, :, my_rows, pl.ds(128 * p, 128)],
                at_chan(p), w_sem["x", l, p],
            )

    def weights_y(l):
        load_w[l].wait()
        for p in range(1, 4):
            wait_in(w.at[l, :, my_rows, pl.ds(128 * p, 128)], w_sem["x", l, p])
        for p in range(1, 4):
            w_sem["y", l, p] = pool.take()
            here = w.at[l, :, my_rows, :]
            send(here, here, at_y(p), w_sem["y", l, p])

    def weights_core(l):
        for p in range(1, 4):
            wait_in(w.at[l, :, pl.ds(core * 64 + ((y + 4 - p) % 4) * 16, 16), :], w_sem["y", l, p])
        w_sem["core", l] = pool.take()
        here = w.at[l, :, pl.ds(core * 64, 64), :]
        send(here, here, sibling, w_sem["core", l])

    def weights_wait(l):
        wait_in(w.at[l, :, pl.ds((1 - core) * 64, 64), :], w_sem["core", l])

    rim_sem = {}

    def rims(k, src, pad):
        up, down = pool.take(), pool.take()
        rim_sem[k] = (up, down)
        send(src.at[:, pl.ds(PX - 128, 128), :], pad.at[:, pl.ds(0, 128), :], nxt, up, has_next)
        send(src.at[:, pl.ds(0, 128), :], pad.at[:, pl.ds(128 + PX, 128), :], prev, down, has_prev)

    def rims_wait(k, pad):
        up, down = rim_sem[k]
        pl.when(has_prev)(lambda: wait_in(pad.at[:, pl.ds(0, 128), :], up))
        pl.when(has_next)(lambda: wait_in(pad.at[:, pl.ds(128 + PX, 128), :], down))

    def transpose_act(pad):
        lane = lax.broadcasted_iota(jnp.int32, (128, 128), 1)

        def body(i, carry):
            f, row = i // 10, i % 10
            v = pad[f, pl.ds(row * 128, 128), :].astype(F32)
            a = (v * sigmoid(v)).astype(BF).astype(F32).T
            at = pl.ds(pl.multiple_of(row * 128, 128), 128)
            before = jnp.where(lane == 0, 0.0, pltpu.roll(a, 1, 1))
            after = jnp.where(lane == 127, 0.0, pltpu.roll(a, 127, 1))
            actt[f, pl.ds(0, 128), at] = before.astype(BF)
            actt[f, pl.ds(128, 128), at] = a.astype(BF)
            actt[f, pl.ds(256, 128), at] = after.astype(BF)
            return carry

        lax.fori_loop(0, 20, body, 0)

    def kernel_grad(l, g, f):
        cotangent = g[f, inside, :]
        for r in range(3):
            part = jnp.dot(actt[f, :, pl.ds(128 * r, PX)], cotangent, preferred_element_type=F32)
            for k in range(4):
                block = part[:, 128 * k : 128 * k + 128].reshape(3, 128, 128)
                if f:
                    block = block + red[l, k, pl.ds(3 * r, 3)]
                red[l, k, pl.ds(3 * r, 3)] = block

    def weight_rows(l, r):
        return w[l, pl.ds(3 * r, 3)].reshape(384, 512)

    def join_taps(acc):
        rows = acc.shape[0]
        col = lax.broadcasted_iota(jnp.int32, (rows, 128), 0) % 128
        first = jnp.where(col == 127, 0.0, pltpu.roll(acc[:, 0:128], rows - 1, 0))
        last = jnp.where(col == 0, 0.0, pltpu.roll(acc[:, 256:384], 1, 0))
        return first + acc[:, 128:256] + last

    halo_sem = {}

    def back_halos(l, g, f):
        up, down = pool.take(), pool.take()
        halo_sem[l, f] = (up, down)
        halo_out[l, f, 0] = join_taps(nt_dot(g[f, pl.ds(128, 128), :], weight_rows(l, 0)))
        halo_out[l, f, 1] = join_taps(nt_dot(g[f, pl.ds(PX, 128), :], weight_rows(l, 2)))
        send(halo_out.at[l, f, 0], halo_in.at[l, f, 1], prev, down, has_prev)
        send(halo_out.at[l, f, 1], halo_in.at[l, f, 0], nxt, up, has_next)

    def back_rows(l, g, f):
        def body(i, carry):
            start = i * 256
            acc = jnp.zeros((256, 384), F32)
            for r in range(3):
                rows = pl.ds(pl.multiple_of(start + (2 - r) * 128, 128), 256)
                acc = acc + nt_dot(g[f, rows, :], weight_rows(l, r))
            back[pl.ds(pl.multiple_of(start, 128), 256), :] = join_taps(acc)
            return carry

        lax.fori_loop(0, 4, body, 0)

    def halos_add(l, f):
        up, down = halo_sem[l, f]

        @pl.when(has_prev)
        def _():
            wait_in(halo_in.at[l, f, 0], up)
            back[pl.ds(0, 128), :] = back[pl.ds(0, 128), :] + halo_in[l, f, 0]

        @pl.when(has_next)
        def _():
            wait_in(halo_in.at[l, f, 1], down)
            back[pl.ds(PX - 128, 128), :] = back[pl.ds(PX - 128, 128), :] + halo_in[l, f, 1]

    def middle_grad(f):
        def body(i, carry):
            rows = pl.ds(pl.multiple_of(i * 128, 128), 128)
            padded = pl.ds(pl.multiple_of(i * 128 + 128, 128), 128)
            v = midpad[f, padded, :].astype(F32)
            gmg[f, padded, pl.ds(0, 128)] = (back[rows, :] * dsilu(v)).astype(BF)
            return carry

        lax.fori_loop(0, 8, body, 0)

    def input_grad(f):
        def body(i, carry):
            rows = pl.ds(pl.multiple_of(i * 128, 128), 128)
            padded = pl.ds(pl.multiple_of(i * 128 + 128, 128), 128)
            v = xpad[f, padded, :].astype(F32)
            og = gog[f, padded, pl.ds(0, 128)].astype(F32)
            ig_buf[f, rows, :] = (og + back[rows, :] * dsilu(v)).astype(BF)
            return carry

        lax.fori_loop(0, 8, body, 0)

    r_sem = {}

    def slot_of(block):
        return (chan + 4 - block) % 4

    def reduce_core(l):
        for h in range(2):
            r_sem["core", l, h] = pool.take()
            send(red.at[l, slot_of(2 * h + 1 - core)], core_in.at[l, h], sibling, r_sem["core", l, h])

    def reduce_y(l):
        for h in range(2):
            wait_in(core_in.at[l, h], r_sem["core", l, h])
            k = slot_of(2 * h + core)

            def body(t, carry):
                total = (red[l, k, t] + core_in[l, h, t]).reshape(4, 4, 8, 128)
                for q in range(4):
                    ysend[l, q, h, t] = total[:, q].reshape(32, 128).astype(BF)
                return carry

            lax.fori_loop(0, 9, body, 0)
        for p in range(1, 4):
            r_sem["y", l, p] = pool.take()
            send(ysend.at[l, (y + p) % 4], yrecv.at[l, p - 1], at_y(p), r_sem["y", l, p])

    def reduce_z(l):
        for p in range(1, 4):
            wait_in(yrecv.at[l, p - 1], r_sem["y", l, p])

        def body(h, carry):
            total = ysend[l, y, h].astype(F32)
            for p in range(3):
                total = total + yrecv[l, p, h].astype(F32)
            total = total.reshape(9, 4, 8, 128)
            for q in range(4):
                rows = jnp.concatenate([total[:, q].reshape(72, 128), jnp.zeros((8, 128), F32)], axis=0)
                zsend[l, h * 4 + q] = rows.astype(BF)
            return carry

        lax.fori_loop(0, 2, body, 0)
        for p in range(1, 8):
            r_sem["z", l, p] = pool.take()
            send(zsend.at[l, (z + p) % 8], zrecv.at[l, p - 1], at_z(p), r_sem["z", l, p])

    def reduce_owner(l):
        for p in range(1, 8):
            wait_in(zrecv.at[l, p - 1], r_sem["z", l, p])
        total = zsend[l, z].astype(F32)
        for p in range(7):
            total = total + zrecv[l, p].astype(F32)
        perm_src[l] = total[0:72].reshape(9, 8, 128)
        r_sem["own", l] = pool.take()
        send(perm_src.at[l], perm_dst.at[l], mirror, r_sem["own", l], crosses)

        @pl.when(jnp.logical_not(crosses))
        def _():
            perm_dst[l] = perm_src[l]

    a_sem = {}

    def adam(l):
        if l == 1:
            for copy in load_adam:
                copy.wait()
        pl.when(crosses)(lambda: wait_in(perm_dst.at[l], r_sem["own", l]))
        grads = perm_dst[l]
        new_moment = 0.9 * adam_in[1, l] + 0.1 * grads
        new_second = 0.999 * adam_in[2, l] + 0.001 * grads * grads
        corrected = new_moment / (1.0 - 0.9**10)
        scale_term = jnp.sqrt(new_second / (1.0 - 0.999**10)) + 1e-08
        new_master = adam_in[0, l] - 0.01 * corrected / scale_term
        adam_out[0, l] = new_master
        adam_out[1, l] = new_moment
        adam_out[2, l] = new_second
        rows = jnp.concatenate([new_master.reshape(72, 128), jnp.zeros((8, 128), F32)], axis=0)
        slabs[l, dp, space] = rows.astype(BF)
        here = slabs.at[l, dp, space]
        for p in range(1, 8):
            a_sem["z", l, p] = pool.take()
            send(here, here, at_z(p), a_sem["z", l, p])

    def spread_y(l):
        for p in range(1, 8):
            other = (z + 8 - p) % 8
            wait_in(slabs.at[l, (other // 4) * 2 + core, (other % 4) * 4 + y], a_sem["z", l, p])
        for p in range(1, 4):
            for q in range(8):
                a_sem["y", l, p, q] = pool.take()
                here = slabs.at[l, (q // 4) * 2 + core, (q % 4) * 4 + y]
                send(here, here, at_y(p), a_sem["y", l, p, q])

    def spread_core(l):
        for p in range(1, 4):
            for q in range(8):
                other = (y + 4 - p) % 4
                wait_in(slabs.at[l, (q // 4) * 2 + core, (q % 4) * 4 + other], a_sem["y", l, p, q])
        for h in range(2):
            a_sem["core", l, h] = pool.take()
            here = slabs.at[l, h * 2 + core]
            send(here, here, sibling, a_sem["core", l, h])

    def spread_wait(l):
        for h in range(2):
            wait_in(slabs.at[l, h * 2 + 1 - core], a_sem["core", l, h])

    def og_half(f, h):
        return og_in.at[f, pl.ds(512 * h, 512), :]

    def mg_half(f, h):
        return gmg.at[(*half(f, h), pl.ds(0, 128))]

    weights_chan(1)
    gather_own("og", gog, og_half, 0)
    rims("mid", mid_in, midpad)
    rims("x", x_in, xpad)
    weights_y(1)
    gather_forward("og", gog, 0)
    weights_chan(0)
    gather_own("og", gog, og_half, 1)
    load_mid.wait()
    rims_wait("mid", midpad)
    transpose_act(midpad)
    weights_core(1)
    weights_y(0)
    gather_wait("og", gog, 0)
    load_og.wait()
    weights_wait(1)
    back_halos(1, gog, 0)
    back_rows(1, gog, 0)
    gather_forward("og", gog, 1)
    halos_add(1, 0)
    middle_grad(0)
    gather_own("mg", gmg, mg_half, 0)
    weights_core(0)
    kernel_grad(1, gog, 0)
    gather_wait("og", gog, 1)
    back_halos(1, gog, 1)
    back_rows(1, gog, 1)
    gather_forward("mg", gmg, 0)
    halos_add(1, 1)
    middle_grad(1)
    gather_own("mg", gmg, mg_half, 1)
    kernel_grad(1, gog, 1)
    reduce_core(1)
    load_x.wait()
    rims_wait("x", xpad)
    transpose_act(xpad)
    reduce_y(1)
    weights_wait(0)
    gather_wait("mg", gmg, 0)
    kernel_grad(0, gmg, 0)
    back_halos(0, gmg, 0)
    back_rows(0, gmg, 0)
    reduce_z(1)
    gather_forward("mg", gmg, 1)
    halos_add(0, 0)
    input_grad(0)
    reduce_owner(1)
    adam(1)
    gather_wait("mg", gmg, 1)
    kernel_grad(0, gmg, 1)
    reduce_core(0)
    spread_y(1)
    back_halos(0, gmg, 1)
    reduce_y(0)
    back_rows(0, gmg, 1)
    reduce_z(0)
    halos_add(0, 1)
    input_grad(1)
    stores = [load(ig_buf, ig_out)]
    spread_core(1)
    reduce_owner(0)
    adam(0)
    stores += [load(adam_out.at[k], ref) for k, ref in enumerate((master_out, moment_out, second_out))]
    spread_y(0)
    spread_wait(1)
    stores.append(load(slabs.at[1], slab_out.at[1]))
    spread_core(0)
    spread_wait(0)
    stores.append(load(slabs.at[0], slab_out.at[0]))
    for copy in stores:
        copy.wait()
    for copy, when in sends:
        if when is None:
            copy.wait_send()
        else:
            pl.when(when)(copy.wait_send)
    assert pool.used <= sems.shape[0], pool.used


def on_device(section_input, middle, out_grad, kernels, master, moment, second):
    any_space = pl.BlockSpec(memory_space=pl.ANY)
    flat = lambda a: a.reshape(2, PX, 128)
    owned = lambda a: a.reshape(2, 9, 8, 128)
    state = jax.ShapeDtypeStruct((2, 9, 8, 128), F32)
    outs = pl.pallas_call(
        kernel,
        out_shape=(
            jax.ShapeDtypeStruct((2, PX, 128), BF),
            jax.ShapeDtypeStruct((2, 4, 16, SLAB, 128), BF),
            state, state, state,
        ),
        in_specs=[any_space] * 7,
        out_specs=[any_space] * 5,
        scratch_shapes=[
            pltpu.VMEM((2, PX + 256, 128), BF),
            pltpu.VMEM((2, PX + 256, 128), BF),
            pltpu.VMEM((2, PX + 256, 512), BF),
            pltpu.VMEM((2, PX + 256, 512), BF),
            pltpu.VMEM((2, 9, 128, 512), BF),
            pltpu.VMEM((2, 384, PX + 256), BF),
            pltpu.VMEM((2, 4, 9, 128, 128), F32),
            pltpu.VMEM((PX, 128), F32),
            pltpu.VMEM((2, 2, 2, 128, 128), F32),
            pltpu.VMEM((2, 2, 2, 128, 128), F32),
            pltpu.VMEM((2, 2, 9, 128, 128), F32),
            pltpu.VMEM((2, 4, 2, 9, 32, 128), BF),
            pltpu.VMEM((2, 3, 2, 9, 32, 128), BF),
            pltpu.VMEM((2, 8, SLAB, 128), BF),
            pltpu.VMEM((2, 7, SLAB, 128), BF),
            pltpu.VMEM((2, 9, 8, 128), F32),
            pltpu.VMEM((2, 9, 8, 128), F32),
            pltpu.VMEM((3, 2, 9, 8, 128), F32),
            pltpu.VMEM((3, 2, 9, 8, 128), F32),
            pltpu.VMEM((2, 4, 16, SLAB, 128), BF),
            pltpu.VMEM((2, PX, 128), BF),
            pltpu.SemaphoreType.DMA((400,)),
        ],
        compiler_params=pltpu.CompilerParams(
            collective_id=0, has_side_effects=True, vmem_limit_bytes=VMEM_LIMIT
        ),
        cost_estimate=pl.CostEstimate(flops=10**10, bytes_accessed=10**7, transcendentals=10**6),
    )(
        flat(section_input), flat(middle), flat(out_grad),
        kernels.reshape(2, 9, 512, 128), owned(master), owned(moment), owned(second),
    )
    input_grad, slabs, new_master, new_moment, new_second = outs
    new_kernels = slabs[:, :, :, 0:72, :].reshape(2, 64, 9, 8, 128).transpose(0, 2, 1, 3, 4)
    back_shape = lambda a: a.reshape(master.shape)
    return (
        input_grad.reshape(section_input.shape),
        new_kernels.reshape(kernels.shape),
        back_shape(new_master), back_shape(new_moment), back_shape(new_second),
    )


def solution(mesh):
    activation = P("dp", None, "space", None, "chan")
    state = P(None, None, None, ("dp", "space"), "chan")
    weights = P(None, None, None, None, "chan")
    return jax.shard_map(
        on_device,
        mesh=mesh,
        in_specs=(activation, activation, activation, weights, state, state, state),
        out_specs=(activation, weights, state, state, state),
        check_vma=False,
    )
```

time: 641 us -> 131 us (0.20)
  waiting for transfers between devices: 516 us -> 0 us
  Pallas kernels: 0 us -> 124 us
  matrix products: 78 us -> 0 us
  between operations: 14.4 us -> 0.69 us
  other arithmetic: 11.8 us -> 0 us
  starting transfers between devices: 10.5 us -> 0 us
    all_gather x3 -> x0, waiting for transfers between devices: 211 us -> none  [the longest x1 152 us: on_device(): lax.all_gather(new_master.astype(jnp.bfloat16), ('dp', 'space'), axis=3,...]
    psum x1 -> x0, waiting for transfers between devices: 197 us -> none  [on_device(): totals = lax.psum(grads, ('dp', 'space'))]
    pallas_call x0 -> x1, Pallas kernels: none -> 124 us  [on_device(): pl.pallas_call(kernel, out_shape=(jax.ShapeDtypeStruct((2, PX, 128), BF),...]
    reduce_scatter x2 -> x0, waiting for transfers between devices: 106 us -> none  [conv_back(): lax.psum_scatter(partial_value, 'chan', scatter_dimension=4, tiled=True)]
    dot_general x36 -> x0, matrix products: 78 us -> none  [the longest x18 54.8 us: conv_back(): lax.dot_general(views[tap], weight[tap // 3, tap % 3], (((1,), (1,)), (()...]
    ppermute x4 -> x0, starting transfers between devices: 10 us -> none  [the longest x2 7.14 us: with_halo(): before = lax.ppermute(last, axis, up)]
    convert_element_type x3 -> x0, other arithmetic: 7.02 us -> none  [the longest x1 2.91 us: on_device(): act1 = jax.nn.silu(in_f).astype(jnp.bfloat16)]
  transfers between devices with their start and end apart: 10 -> 0, of which waited for: 8 -> 0; matrix products, arithmetic and copies ran while one was open for 4% -> 0% of each run, Pallas kernels for 0% -> 0%
where the time goes in v1:
time: 131 us
  Pallas kernels  124 us (95%)
  local copies, waits for them, and re-layouts  6.64 us (5%)
    pallas_call x1, Pallas kernels, on_device(): pl.pallas_call(kernel, out_shape=(jax.ShapeDtypeStruct((2, PX, 128), BF),...  124 us
    unnamed x12, local copies, waits for them, and re-layouts  2.71 us

profile of v1, /device:TPU:1, one launch (start us, length us, event | category | flops | bytes accessed | tf_op | source)
XLA Modules:
  0.0 131.0 jit_solution(9522731150032426919)
XLA Ops:
  0.6 123.6 %shard_map.110 = (bf16[2,1024,128]{2,1,0:T(8,128)(2,1)}, bf16[2,4,16,80,128]{4,3,2,1,0:T(8,128)(2,1)}, f32[2,9,8,128]{3,2,1,0:T(8,128)}, f32[2,9,8,128]{3,2,1,0:T(8,128)}, f32[2,9,8,128]{3,2,1,0:T(8,128)}) custom-call(bf16[2,1024,128]{2,1,0:T(8,128)(2,1)} %bitcast.22, bf16[2,1024,128]{2,1,0:T(8,128)(2,1)} %bitcast.23, bf16[2,1024,128]{2,1,0:T(8,128)(2,1)} %bitcast.24, ...), custom_call_target="tpu_custom_call" | custom-call | flops 10000000000 | bytes 10000000 | tf_op jit(solution)/shard_map/pallas_call | solution.py:501
  124.3 1.9 %slice.3 = bf16[2,4,16,72,128]{4,3,2,1,0:T(8,128)(2,1)S(1)} slice(bf16[2,4,16,80,128]{4,3,2,1,0:T(8,128)(2,1)} %get-tuple-element.11), slice={[0:2], [0:4], [0:16], [0:72], [0:128]} | slice | bytes 4718592 | tf_op jit(solution)/shard_map/slice | solution.py:543
  126.2 0.0 copy-start
  126.2 0.0 copy-start.3
  126.2 0.0 copy-start.2
  126.2 0.0 copy-start.1
  126.2 2.0 %copy.12 = bf16[2,9,64,8,128]{4,3,2,1,0:T(8,128)(2,1)} copy(bf16[2,9,64,8,128]{4,3,1,2,0:T(8,128)(2,1)S(1)} %bitcast.15) | data formatting | bytes 4718592 | tf_op jit(solution)/shard_map/transpose | solution.py:543
  128.2 0.0 copy-done
  128.2 0.8 copy.17
  129.0 0.0 copy-done.3
  129.0 0.6 copy.18
  129.7 0.0 copy-done.2
  129.7 0.6 copy.19
  130.3 0.0 copy-done.1
  130.3 0.6 copy.20
Async XLA Ops:
  126.2 2.1 %copy-start = (bf16[2,1024,128]{2,1,0:T(8,128)(2,1)S(1)}, bf16[2,1024,128]{2,1,0:T(8,128)(2,1)}, u32[]{:S(2)}) copy-start(bf16[2,1024,128]{2,1,0:T(8,128)(2,1)} %get-tuple-element.10) | copy-start | bytes 1572868
  126.2 2.9 %copy-start.3 = (f32[2,9,8,128]{3,2,1,0:T(8,128)S(1)}, f32[2,9,8,128]{3,2,1,0:T(8,128)}, u32[]{:S(2)}) copy-start(f32[2,9,8,128]{3,2,1,0:T(8,128)} %get-tuple-element.12) | copy-start | bytes 221188
  126.2 3.5 %copy-start.2 = (f32[2,9,8,128]{3,2,1,0:T(8,128)S(1)}, f32[2,9,8,128]{3,2,1,0:T(8,128)}, u32[]{:S(2)}) copy-start(f32[2,9,8,128]{3,2,1,0:T(8,128)} %get-tuple-element.13) | copy-start | bytes 221188
  126.2 4.1 %copy-start.1 = (f32[2,9,8,128]{3,2,1,0:T(8,128)S(1)}, f32[2,9,8,128]{3,2,1,0:T(8,128)}, u32[]{:S(2)}) copy-start(f32[2,9,8,128]{3,2,1,0:T(8,128)} %get-tuple-element.14) | copy-start | bytes 221188

commit v2 on v1

--- a/solution.py
+++ b/solution.py
@@ -10,6 +10,7 @@
 MESH = pl.DeviceIdType.MESH
 PX = 1024
 SLAB = 80
+SEMS = 440
 VMEM_LIMIT = 56 * 1024 * 1024
 
 
@@ -39,9 +40,9 @@
 
 def kernel(
     x_in, mid_in, og_in, kern, master, moment, second,
-    ig_out, slab_out, master_out, moment_out, second_out,
+    ig_out, kern_out, master_out, moment_out, second_out,
     xpad, midpad, gog, gmg, w, actt, red, back, halo_in, halo_out, core_in,
-    ysend, yrecv, zsend, zrecv, perm_src, perm_dst, adam_in, adam_out, slabs, ig_buf, sems,
+    ysend, yrecv, zsend, zrecv, adam_in, adam_out, slabs, new_kern, ig_buf, sems,
 ):
     chan = lax.axis_index("chan")
     dp = lax.axis_index("dp")
@@ -63,10 +64,9 @@
         return {"dp": (other // 4) * 2 + core, "space": (other % 4) * 4 + y}
 
     sibling = {"dp": z_hi * 2 + (1 - core)}
-    mirror = {"dp": chan, "chan": dp}
     has_prev = space > 0
     has_next = space < 15
-    crosses = chan != dp
+    on_diagonal = chan == dp
 
     def send(src, dst, target, recv_sem, when=None):
         copy = pltpu.make_async_remote_copy(
@@ -112,7 +112,9 @@
     prev, nxt = {"space": space - 1}, {"space": space + 1}
     pl.when(has_prev)(lambda: greet(prev))
     pl.when(has_next)(lambda: greet(nxt))
-    pl.when(crosses)(lambda: greet(mirror))
+    for q in range(8):
+        source = {"dp": (q // 4) * 2 + chan % 2, "chan": dp, "space": (q % 4) * 4 + y}
+        pl.when(jnp.logical_not(on_diagonal & (z == q)))(lambda source=source: greet(source))
 
     zero_row = jnp.zeros((128, 512), BF)
     for g in (gog, gmg):
@@ -130,7 +132,7 @@
         for pad in (midpad, xpad):
             pad[:, pl.ds(128 + PX, 128), :] = jnp.zeros((2, 128, 128), BF)
 
-    expected = 14 + has_prev.astype(jnp.int32) + has_next.astype(jnp.int32) + crosses.astype(jnp.int32)
+    expected = 22 + has_prev.astype(jnp.int32) + has_next.astype(jnp.int32) - on_diagonal.astype(jnp.int32)
     pl.semaphore_wait(barrier, expected)
 
     gathers = {}
@@ -187,14 +189,16 @@
             send(here, here, at_y(p), w_sem["y", l, p])
 
     def weights_core(l):
-        for p in range(1, 4):
-            wait_in(w.at[l, :, pl.ds(core * 64 + ((y + 4 - p) % 4) * 16, 16), :], w_sem["y", l, p])
-        w_sem["core", l] = pool.take()
-        here = w.at[l, :, pl.ds(core * 64, 64), :]
-        send(here, here, sibling, w_sem["core", l])
+        for p in range(4):
+            if p:
+                wait_in(w.at[l, :, pl.ds(core * 64 + ((y + 4 - p) % 4) * 16, 16), :], w_sem["y", l, p])
+            w_sem["core", l, p] = pool.take()
+            here = w.at[l, :, pl.ds(core * 64 + ((y + 4 - p) % 4) * 16, 16), :]
+            send(here, here, sibling, w_sem["core", l, p])
 
     def weights_wait(l):
-        wait_in(w.at[l, :, pl.ds((1 - core) * 64, 64), :], w_sem["core", l])
+        for p in range(4):
+            wait_in(w.at[l, :, pl.ds((1 - core) * 64 + ((y + 4 - p) % 4) * 16, 16), :], w_sem["core", l, p])
 
     rim_sem = {}
 
@@ -312,101 +316,122 @@
             r_sem["core", l, h] = pool.take()
             send(red.at[l, slot_of(2 * h + 1 - core)], core_in.at[l, h], sibling, r_sem["core", l, h])
 
+    def as_slab(v):
+        return jnp.concatenate([v.reshape(72, 128), jnp.zeros((8, 128), F32)], axis=0).astype(BF)
+
+    near_last = (2, 3, 1, 0)
+
     def reduce_y(l):
         for h in range(2):
             wait_in(core_in.at[l, h], r_sem["core", l, h])
-            k = slot_of(2 * h + core)
-
-            def body(t, carry):
-                total = (red[l, k, t] + core_in[l, h, t]).reshape(4, 4, 8, 128)
-                for q in range(4):
-                    ysend[l, q, h, t] = total[:, q].reshape(32, 128).astype(BF)
+        for p in (2, 1, 3, 0):
+            q = (y + p) % 4
+
+            def body(c, carry, q=q):
+                rows = pl.ds(pl.multiple_of(c * 32 + q * 8, 8), 8)
+                for h in range(2):
+                    total = red[l, slot_of(2 * h + core), :, rows, :] + core_in[l, h, :, rows, :]
+                    ysend[l, q, c, h] = as_slab(total)
                 return carry
 
-            lax.fori_loop(0, 9, body, 0)
-        for p in range(1, 4):
-            r_sem["y", l, p] = pool.take()
-            send(ysend.at[l, (y + p) % 4], yrecv.at[l, p - 1], at_y(p), r_sem["y", l, p])
+            lax.fori_loop(0, 4, body, 0)
+            if p:
+                for j in near_last:
+                    r_sem["y", l, p, j] = pool.take()
+                    send(ysend.at[l, q, (z_lo + j) % 4], yrecv.at[l, p - 1, j], at_y(p), r_sem["y", l, p, j])
 
     def reduce_z(l):
-        for p in range(1, 4):
-            wait_in(yrecv.at[l, p - 1], r_sem["y", l, p])
-
-        def body(h, carry):
-            total = ysend[l, y, h].astype(F32)
-            for p in range(3):
-                total = total + yrecv[l, p, h].astype(F32)
-            total = total.reshape(9, 4, 8, 128)
-            for q in range(4):
-                rows = jnp.concatenate([total[:, q].reshape(72, 128), jnp.zeros((8, 128), F32)], axis=0)
-                zsend[l, h * 4 + q] = rows.astype(BF)
-            return carry
-
-        lax.fori_loop(0, 2, body, 0)
-        for p in range(1, 8):
-            r_sem["z", l, p] = pool.take()
-            send(zsend.at[l, (z + p) % 8], zrecv.at[l, p - 1], at_z(p), r_sem["z", l, p])
-
-    def reduce_owner(l):
-        for p in range(1, 8):
-            wait_in(zrecv.at[l, p - 1], r_sem["z", l, p])
-        total = zsend[l, z].astype(F32)
-        for p in range(7):
-            total = total + zrecv[l, p].astype(F32)
-        perm_src[l] = total[0:72].reshape(9, 8, 128)
-        r_sem["own", l] = pool.take()
-        send(perm_src.at[l], perm_dst.at[l], mirror, r_sem["own", l], crosses)
-
-        @pl.when(jnp.logical_not(crosses))
-        def _():
-            perm_dst[l] = perm_src[l]
+        r_sem["z", l] = pool.take(8)
+        for j in near_last:
+            c = (z_lo + j) % 4
+            for p in range(1, 4):
+                wait_in(yrecv.at[l, p - 1, j], r_sem["y", l, p, j])
+            for h in range(2):
+                total = ysend[l, y, c, h].astype(F32)
+                for p in range(3):
+                    total = total + yrecv[l, p, j, h].astype(F32)
+                total = total.astype(BF)
+                zsend[l, j, h] = total
+                owner = {"chan": 2 * h + core, "dp": chan, "space": c * 4 + y}
+                mine = on_diagonal & (z_hi == h)
+                away = jnp.logical_not(mine) if j == 0 else None
+                send(zsend.at[l, j, h], zrecv.at[l, z], owner, r_sem["z", l] + z, away)
+                if j == 0:
+
+                    @pl.when(mine)
+                    def _(total=total):
+                        zrecv[l, z] = total
 
     a_sem = {}
+    by_distance = (0, 1, 7, 2, 6, 3, 5, 4)
+
+    def z_from(d):
+        other = (z + 8 - d) % 8
+        return (other // 4) * 2 + core, other % 4
 
     def adam(l):
         if l == 1:
             for copy in load_adam:
                 copy.wait()
-        pl.when(crosses)(lambda: wait_in(perm_dst.at[l], r_sem["own", l]))
-        grads = perm_dst[l]
+        for q in range(8):
+            there = jnp.logical_not(on_diagonal & (z == q))
+            pl.when(there)(lambda q=q: wait_in(zrecv.at[l, q], r_sem["z", l] + q))
+        grads = zrecv[l, 0].astype(F32)
+        for q in range(1, 8):
+            grads = grads + zrecv[l, q].astype(F32)
+        grads = grads[0:72].reshape(9, 8, 128)
         new_moment = 0.9 * adam_in[1, l] + 0.1 * grads
         new_second = 0.999 * adam_in[2, l] + 0.001 * grads * grads
         corrected = new_moment / (1.0 - 0.9**10)
         scale_term = jnp.sqrt(new_second / (1.0 - 0.999**10)) + 1e-08
         new_master = adam_in[0, l] - 0.01 * corrected / scale_term
+        slabs[l, dp, space] = as_slab(new_master)
+        here = slabs.at[l, dp, space]
+        for p in by_distance[1:]:
+            a_sem["z", l, p] = pool.take()
+            send(here, here, at_z(p), a_sem["z", l, p])
+        to_y(l, 0)
         adam_out[0, l] = new_master
         adam_out[1, l] = new_moment
         adam_out[2, l] = new_second
-        rows = jnp.concatenate([new_master.reshape(72, 128), jnp.zeros((8, 128), F32)], axis=0)
-        slabs[l, dp, space] = rows.astype(BF)
-        here = slabs.at[l, dp, space]
-        for p in range(1, 8):
-            a_sem["z", l, p] = pool.take()
-            send(here, here, at_z(p), a_sem["z", l, p])
+
+    def to_y(l, d):
+        dp_there, z_there = z_from(d)
+        here = slabs.at[l, dp_there, z_there * 4 + y]
+        for p in range(1, 4):
+            a_sem["y", l, p, d] = pool.take()
+            send(here, here, at_y(p), a_sem["y", l, p, d])
 
     def spread_y(l):
-        for p in range(1, 8):
-            other = (z + 8 - p) % 8
-            wait_in(slabs.at[l, (other // 4) * 2 + core, (other % 4) * 4 + y], a_sem["z", l, p])
-        for p in range(1, 4):
-            for q in range(8):
-                a_sem["y", l, p, q] = pool.take()
-                here = slabs.at[l, (q // 4) * 2 + core, (q % 4) * 4 + y]
-                send(here, here, at_y(p), a_sem["y", l, p, q])
+        for d in by_distance[1:]:
+            dp_there, z_there = z_from(d)
+            wait_in(slabs.at[l, dp_there, z_there * 4 + y], a_sem["z", l, d])
+            to_y(l, d)
+
+    def assemble(l, dp_there, z_there):
+        for pair in range(2):
+            both = [
+                slabs[l, dp_there, z_there * 4 + 2 * pair + i].astype(F32)[0:72].reshape(9, 8, 128) for i in range(2)
+            ]
+            rows = pl.ds(pl.multiple_of(dp_there * 128 + z_there * 32 + pair * 16, 16), 16)
+            new_kern[l, :, rows, :] = jnp.concatenate(both, axis=1).astype(BF)
 
     def spread_core(l):
-        for p in range(1, 4):
-            for q in range(8):
-                other = (y + 4 - p) % 4
-                wait_in(slabs.at[l, (q // 4) * 2 + core, (q % 4) * 4 + other], a_sem["y", l, p, q])
-        for h in range(2):
-            a_sem["core", l, h] = pool.take()
-            here = slabs.at[l, h * 2 + core]
-            send(here, here, sibling, a_sem["core", l, h])
+        for d in by_distance:
+            dp_there, z_there = z_from(d)
+            for p in range(1, 4):
+                wait_in(slabs.at[l, dp_there, z_there * 4 + (y + 4 - p) % 4], a_sem["y", l, p, d])
+            a_sem["core", l, d] = pool.take()
+            here = slabs.at[l, dp_there, pl.ds(z_there * 4, 4)]
+            send(here, here, sibling, a_sem["core", l, d])
+            assemble(l, dp_there, z_there)
 
     def spread_wait(l):
-        for h in range(2):
-            wait_in(slabs.at[l, h * 2 + 1 - core], a_sem["core", l, h])
+        for d in by_distance:
+            dp_there, z_there = z_from(d)
+            dp_there = dp_there + 1 - 2 * core
+            wait_in(slabs.at[l, dp_there, pl.ds(z_there * 4, 4)], a_sem["core", l, d])
+            assemble(l, dp_there, z_there)
 
     def og_half(f, h):
         return og_in.at[f, pl.ds(512 * h, 512), :]
@@ -417,7 +442,6 @@
     weights_chan(1)
     gather_own("og", gog, og_half, 0)
     rims("mid", mid_in, midpad)
-    rims("x", x_in, xpad)
     weights_y(1)
     gather_forward("og", gog, 0)
     weights_chan(0)
@@ -425,64 +449,63 @@
     load_mid.wait()
     rims_wait("mid", midpad)
     transpose_act(midpad)
-    weights_core(1)
-    weights_y(0)
     gather_wait("og", gog, 0)
     load_og.wait()
+    kernel_grad(1, gog, 0)
+    gather_forward("og", gog, 1)
+    weights_core(1)
+    rims("x", x_in, xpad)
+    weights_y(0)
     weights_wait(1)
     back_halos(1, gog, 0)
     back_rows(1, gog, 0)
-    gather_forward("og", gog, 1)
     halos_add(1, 0)
     middle_grad(0)
     gather_own("mg", gmg, mg_half, 0)
-    weights_core(0)
-    kernel_grad(1, gog, 0)
     gather_wait("og", gog, 1)
     back_halos(1, gog, 1)
+    kernel_grad(1, gog, 1)
+    reduce_core(1)
     back_rows(1, gog, 1)
     gather_forward("mg", gmg, 0)
     halos_add(1, 1)
     middle_grad(1)
     gather_own("mg", gmg, mg_half, 1)
-    kernel_grad(1, gog, 1)
-    reduce_core(1)
+    reduce_y(1)
+    weights_core(0)
     load_x.wait()
     rims_wait("x", xpad)
     transpose_act(xpad)
-    reduce_y(1)
     weights_wait(0)
     gather_wait("mg", gmg, 0)
     kernel_grad(0, gmg, 0)
+    gather_forward("mg", gmg, 1)
     back_halos(0, gmg, 0)
     back_rows(0, gmg, 0)
     reduce_z(1)
-    gather_forward("mg", gmg, 1)
     halos_add(0, 0)
     input_grad(0)
-    reduce_owner(1)
-    adam(1)
     gather_wait("mg", gmg, 1)
     kernel_grad(0, gmg, 1)
     reduce_core(0)
-    spread_y(1)
     back_halos(0, gmg, 1)
     reduce_y(0)
+    adam(1)
     back_rows(0, gmg, 1)
-    reduce_z(0)
     halos_add(0, 1)
     input_grad(1)
     stores = [load(ig_buf, ig_out)]
-    spread_core(1)
-    reduce_owner(0)
+    reduce_z(0)
+    spread_y(1)
     adam(0)
     stores += [load(adam_out.at[k], ref) for k, ref in enumerate((master_out, moment_out, second_out))]
+    spread_core(1)
     spread_y(0)
     spread_wait(1)
-    stores.append(load(slabs.at[1], slab_out.at[1]))
+    stores.append(load(new_kern.at[1], kern_out.at[1]))
     spread_core(0)
     spread_wait(0)
-    stores.append(load(slabs.at[0], slab_out.at[0]))
+    stores.append(load(new_kern.at[0], kern_out.at[0]))
     for copy in stores:
         copy.wait()
     for copy, when in sends:
@@ -493,18 +516,37 @@
     assert pool.used <= sems.shape[0], pool.used
 
 
+def hand_over(ig, kern, master, moment, second, *refs):
+    outs, held, sems = refs[:5], refs[5:10], refs[10]
+    parts = [(1, (l, pl.ds(3 * r, 3))) for l in range(2) for r in range(3)]
+    parts += [(0, (f,)) for f in range(2)] + [(k, (l,)) for k in (2, 3, 4) for l in range(2)]
+    ins = (ig, kern, master, moment, second)
+    steps = []
+    for i, (k, at) in enumerate(parts):
+        arrive = pltpu.make_async_copy(ins[k].at[at], held[k].at[at], sems.at[0, i])
+        leave = pltpu.make_async_copy(held[k].at[at], outs[k].at[at], sems.at[1, i])
+        arrive.start()
+        steps.append((arrive, leave))
+    for arrive, leave in steps:
+        arrive.wait()
+        leave.start()
+    for arrive, leave in steps:
+        leave.wait()
+
+
 def on_device(section_input, middle, out_grad, kernels, master, moment, second):
     any_space = pl.BlockSpec(memory_space=pl.ANY)
     flat = lambda a: a.reshape(2, PX, 128)
     owned = lambda a: a.reshape(2, 9, 8, 128)
     state = jax.ShapeDtypeStruct((2, 9, 8, 128), F32)
+    results = (
+        jax.ShapeDtypeStruct((2, PX, 128), BF),
+        jax.ShapeDtypeStruct((2, 9, 512, 128), BF),
+        state, state, state,
+    )
     outs = pl.pallas_call(
         kernel,
-        out_shape=(
-            jax.ShapeDtypeStruct((2, PX, 128), BF),
-            jax.ShapeDtypeStruct((2, 4, 16, SLAB, 128), BF),
-            state, state, state,
-        ),
+        out_shape=results,
         in_specs=[any_space] * 7,
         out_specs=[any_space] * 5,
         scratch_shapes=[
@@ -519,17 +561,16 @@
             pltpu.VMEM((2, 2, 2, 128, 128), F32),
             pltpu.VMEM((2, 2, 2, 128, 128), F32),
             pltpu.VMEM((2, 2, 9, 128, 128), F32),
-            pltpu.VMEM((2, 4, 2, 9, 32, 128), BF),
-            pltpu.VMEM((2, 3, 2, 9, 32, 128), BF),
+            pltpu.VMEM((2, 4, 4, 2, SLAB, 128), BF),
+            pltpu.VMEM((2, 3, 4, 2, SLAB, 128), BF),
+            pltpu.VMEM((2, 4, 2, SLAB, 128), BF),
             pltpu.VMEM((2, 8, SLAB, 128), BF),
-            pltpu.VMEM((2, 7, SLAB, 128), BF),
-            pltpu.VMEM((2, 9, 8, 128), F32),
-            pltpu.VMEM((2, 9, 8, 128), F32),
             pltpu.VMEM((3, 2, 9, 8, 128), F32),
             pltpu.VMEM((3, 2, 9, 8, 128), F32),
             pltpu.VMEM((2, 4, 16, SLAB, 128), BF),
+            pltpu.VMEM((2, 9, 512, 128), BF),
             pltpu.VMEM((2, PX, 128), BF),
-            pltpu.SemaphoreType.DMA((400,)),
+            pltpu.SemaphoreType.DMA((SEMS,)),
         ],
         compiler_params=pltpu.CompilerParams(
             collective_id=0, has_side_effects=True, vmem_limit_bytes=VMEM_LIMIT
@@ -539,14 +580,15 @@
         flat(section_input), flat(middle), flat(out_grad),
         kernels.reshape(2, 9, 512, 128), owned(master), owned(moment), owned(second),
     )
-    input_grad, slabs, new_master, new_moment, new_second = outs
-    new_kernels = slabs[:, :, :, 0:72, :].reshape(2, 64, 9, 8, 128).transpose(0, 2, 1, 3, 4)
-    back_shape = lambda a: a.reshape(master.shape)
-    return (
-        input_grad.reshape(section_input.shape),
-        new_kernels.reshape(kernels.shape),
-        back_shape(new_master), back_shape(new_moment), back_shape(new_second),
-    )
+    outs = pl.pallas_call(
+        hand_over,
+        out_shape=results,
+        in_specs=[any_space] * 5,
+        out_specs=[any_space] * 5,
+        scratch_shapes=[pltpu.VMEM(r.shape, r.dtype) for r in results] + [pltpu.SemaphoreType.DMA((2, 14))],
+    )(*outs)
+    shapes = (section_input.shape, kernels.shape, master.shape, master.shape, master.shape)
+    return tuple(out.reshape(shape) for out, shape in zip(outs, shapes))
 
 
 def solution(mesh):

time: 131 us -> 102 us (0.78)
  Pallas kernels: 124 us -> 101 us
  local copies, waits for them, and re-layouts: 6.64 us -> 0 us
    pallas_call x1 -> x2, Pallas kernels: 124 us -> 101 us  [the longest x1 98.3 us: on_device(): pl.pallas_call(kernel, out_shape=results, in_specs=[any_space] * 7, out_s...]
    unnamed x12 -> x0, local copies, waits for them, and re-layouts: 2.71 us -> none
    transpose x1 -> x0, local copies, waits for them, and re-layouts: 2.03 us -> none  [on_device(): slabs[:, :, :, 0:72, :].reshape(2, 64, 9, 8, 128).transpose(0, 2, 1, 3, 4)]
    slice x1 -> x0, local copies, waits for them, and re-layouts: 1.9 us -> none  [on_device(): slabs[:, :, :, 0:72, :].reshape(2, 64, 9, 8, 128).transpose(0, 2, 1, 3, 4)]
where the time goes in v2:
time: 102 us
  Pallas kernels  101 us (99%)
    pallas_call x1, Pallas kernels, on_device(): pl.pallas_call(kernel, out_shape=results, in_specs=[any_space] * 7, out_s...  98.3 us
    pallas_call x1, Pallas kernels, on_device(): pl.pallas_call(hand_over, out_shape=results, in_specs=[any_space] * 5, ou...  2.87 us

profile of v2, /device:TPU:1, one launch (start us, length us, event | category | flops | bytes accessed | tf_op | source)
XLA Modules:
  0.0 101.8 jit_solution(14579037594145628128)
XLA Ops:
  0.6 98.3 %shard_map.110 = (bf16[2,1024,128]{2,1,0:T(8,128)(2,1)}, bf16[2,9,512,128]{3,2,1,0:T(8,128)(2,1)}, f32[2,9,8,128]{3,2,1,0:T(8,128)}, f32[2,9,8,128]{3,2,1,0:T(8,128)}, f32[2,9,8,128]{3,2,1,0:T(8,128)}) custom-call(bf16[2,1024,128]{2,1,0:T(8,128)(2,1)} %bitcast.14, bf16[2,1024,128]{2,1,0:T(8,128)(2,1)} %bitcast.15, bf16[2,1024,128]{2,1,0:T(8,128)(2,1)} %bitcast.16, ...), custom_call_target="tpu_custom_call" | custom-call | flops 10000000000 | bytes 10000000 | tf_op jit(solution)/shard_map/pallas_call | solution.py:547
  98.9 2.9 %shard_map.111 = (bf16[2,1024,128]{2,1,0:T(8,128)(2,1)}, bf16[2,9,512,128]{3,2,1,0:T(8,128)(2,1)}, f32[2,9,8,128]{3,2,1,0:T(8,128)}, f32[2,9,8,128]{3,2,1,0:T(8,128)}, f32[2,9,8,128]{3,2,1,0:T(8,128)}) custom-call(bf16[2,1024,128]{2,1,0:T(8,128)(2,1)} %get-tuple-element.15.ig, bf16[2,9,512,128]{3,2,1,0:T(8,128)(2,1)} %get-tuple-element.16.kern, ...), custom_call_target="tpu_custom_call" | custom-call | tf_op jit(solution)/shard_map/pallas_call | solution.py:583

commit v3 on v2

--- a/solution.py
+++ b/solution.py
@@ -10,7 +10,7 @@
 MESH = pl.DeviceIdType.MESH
 PX = 1024
 SLAB = 80
-SEMS = 440
+SEMS = 520
 VMEM_LIMIT = 56 * 1024 * 1024
 
 
@@ -42,7 +42,7 @@
     x_in, mid_in, og_in, kern, master, moment, second,
     ig_out, kern_out, master_out, moment_out, second_out,
     xpad, midpad, gog, gmg, w, actt, red, back, halo_in, halo_out, core_in,
-    ysend, yrecv, zsend, zrecv, adam_in, adam_out, slabs, new_kern, ig_buf, sems,
+    ysend, yrecv, zsend, zrecv, adam_in, adam_out, slabs, new_kern, ig_buf, sems, meet,
 ):
     chan = lax.axis_index("chan")
     dp = lax.axis_index("dp")
@@ -58,6 +58,9 @@
 
     def at_y(p):
         return {"space": z_lo * 4 + (y + p) % 4}
+
+    def at_z_lo(p):
+        return {"space": ((z_lo + p) % 4) * 4 + y}
 
     def at_z(p):
         other = (z + p) % 8
@@ -87,118 +90,150 @@
         copy.start()
         return copy
 
+    barrier = pltpu.get_barrier_semaphore()
+
+    def signal(sem, target):
+        pl.semaphore_signal(sem, inc=1, device_id=target, device_id_type=MESH)
+
+    prev, nxt = {"space": space - 1}, {"space": space + 1}
+    first_z, last_z = z_lo == 0, z_lo == 3
+    for p in range(1, 4):
+        signal(barrier, at_chan(p))
+        signal(barrier, at_y(p))
+        signal(barrier, at_z_lo(p))
+    signal(barrier, sibling)
+    pl.when(has_prev)(lambda: signal(barrier, prev))
+    pl.when(has_next)(lambda: signal(barrier, nxt))
+    pl.when(first_z)(lambda: signal(barrier, at_z(7)))
+
     inside = pl.ds(128, PX)
     load_mid = load(mid_in, midpad.at[:, inside, :])
     load_x = load(x_in, xpad.at[:, inside, :])
     load_og = load(og_in, gog.at[:, inside, pl.ds(0, 128)])
-    my_rows = pl.ds(core * 64 + y * 16, 16)
-    load_w = [
-        load(kern.at[l, :, pl.ds(chan * 128 + core * 64 + y * 16, 16), :], w.at[l, :, my_rows, pl.ds(0, 128)])
-        for l in range(2)
-    ]
+    w_parts = ((pl.ds(0, 6), y, at_y), (pl.ds(6, 3), z_lo, at_z_lo))
+
+    def w_rows(index, core=core):
+        return pl.ds(core * 64 + index * 16, 16)
+
+    load_w = {
+        (l, i): load(
+            kern.at[l, taps, pl.ds(chan * 128 + core * 64 + index * 16, 16), :], w.at[l, taps, w_rows(index), pl.ds(0, 128)]
+        )
+        for l in (1, 0)
+        for i, (taps, index, _) in enumerate(w_parts)
+    }
     load_adam = [load(ref, adam_in.at[k]) for k, ref in enumerate((master, moment, second))]
 
-    barrier = pltpu.get_barrier_semaphore()
-
-    def greet(target):
-        pl.semaphore_signal(barrier, inc=1, device_id=target, device_id_type=MESH)
-
-    for p in range(1, 4):
-        greet(at_chan(p))
-        greet(at_y(p))
-    for p in range(1, 8):
-        greet(at_z(p))
-    greet(sibling)
-    prev, nxt = {"space": space - 1}, {"space": space + 1}
-    pl.when(has_prev)(lambda: greet(prev))
-    pl.when(has_next)(lambda: greet(nxt))
-    for q in range(8):
-        source = {"dp": (q // 4) * 2 + chan % 2, "chan": dp, "space": (q % 4) * 4 + y}
-        pl.when(jnp.logical_not(on_diagonal & (z == q)))(lambda source=source: greet(source))
-
-    zero_row = jnp.zeros((128, 512), BF)
-    for g in (gog, gmg):
-        for f in range(2):
-            g[f, pl.ds(0, 128), :] = zero_row
-            g[f, pl.ds(128 + PX, 128), :] = zero_row
-
-    @pl.when(space == 0)
-    def _():
-        for pad in (midpad, xpad):
-            pad[:, pl.ds(0, 128), :] = jnp.zeros((2, 128, 128), BF)
-
-    @pl.when(space == 15)
-    def _():
-        for pad in (midpad, xpad):
-            pad[:, pl.ds(128 + PX, 128), :] = jnp.zeros((2, 128, 128), BF)
-
-    expected = 22 + has_prev.astype(jnp.int32) + has_next.astype(jnp.int32) - on_diagonal.astype(jnp.int32)
+
+    expected = 10 + has_prev.astype(jnp.int32) + has_next.astype(jnp.int32) + last_z.astype(jnp.int32)
     pl.semaphore_wait(barrier, expected)
 
+    def hear_half():
+        pl.when(last_z)(lambda: signal(meet.at[0], at_z(1)))
+
+    def hear_ring():
+        @pl.when(first_z)
+        def _():
+            pl.semaphore_wait(meet.at[0], 1)
+            for p in range(1, 4):
+                signal(meet.at[1], at_z_lo(p))
+
+    def hear_sibling():
+        pl.when(jnp.logical_not(first_z))(lambda: pl.semaphore_wait(meet.at[1], 1))
+        signal(meet.at[2], sibling)
+
+    def hear_chan():
+        pl.semaphore_wait(meet.at[2], 1)
+        for p in range(1, 4):
+            signal(meet.at[3], at_chan(p))
+
+    def hear_all():
+        pl.semaphore_wait(meet.at[3], 3)
+
+    def clear_edges():
+        zero_row = jnp.zeros((128, 512), BF)
+        for g in (gog, gmg):
+            for f in range(2):
+                g[f, pl.ds(0, 128), :] = zero_row
+                g[f, pl.ds(128 + PX, 128), :] = zero_row
+
+        @pl.when(space == 0)
+        def _():
+            for pad in (midpad, xpad):
+                pad[:, pl.ds(0, 128), :] = jnp.zeros((2, 128, 128), BF)
+
+        @pl.when(space == 15)
+        def _():
+            for pad in (midpad, xpad):
+                pad[:, pl.ds(128 + PX, 128), :] = jnp.zeros((2, 128, 128), BF)
+
     gathers = {}
 
-    def half(f, h):
-        return (f, pl.ds(128 + 512 * h, 512))
-
-    def gather_own(name, g, src, f):
+    pieces = range(4)
+
+    def piece(f, i):
+        return (f, pl.ds(128 + 256 * i, 256))
+
+    def gather_own(name, g, src, f, order):
         sem = gathers.setdefault(name, {})
-        for k in ("left", "right", "far"):
-            for h in range(2):
-                sem[k, f, h] = pool.take()
-        for step in range(2):
-            h = step
-            send(src(f, h), g.at[(*half(f, h), pl.ds(128, 128))], at_chan(1), sem["left", f, h])
-            h = 1 - step
-            send(src(f, h), g.at[(*half(f, h), pl.ds(384, 128))], at_chan(3), sem["right", f, h])
-
-    def gather_forward(name, g, f):
+        for i in order:
+            for k in ("left", "right", "far"):
+                sem[k, f, i] = pool.take()
+        for i, j in zip(order, tuple(order)[::-1]):
+            send(src(f, i), g.at[(*piece(f, i), pl.ds(128, 128))], at_chan(1), sem["left", f, i])
+            send(src(f, j), g.at[(*piece(f, j), pl.ds(384, 128))], at_chan(3), sem["right", f, j])
+
+    def gather_forward(name, g, f, order):
         sem = gathers[name]
-        here = g.at[(*half(f, 0), pl.ds(128, 128))]
-        wait_in(here, sem["left", f, 0])
-        send(here, g.at[(*half(f, 0), pl.ds(256, 128))], at_chan(1), sem["far", f, 0])
-        here = g.at[(*half(f, 1), pl.ds(384, 128))]
-        wait_in(here, sem["right", f, 1])
-        send(here, g.at[(*half(f, 1), pl.ds(256, 128))], at_chan(3), sem["far", f, 1])
+        for i in order:
+            k, lanes, target = ("left", 128, at_chan(1)) if i < 2 else ("right", 384, at_chan(3))
+            here = g.at[(*piece(f, i), pl.ds(lanes, 128))]
+            wait_in(here, sem[k, f, i])
+            send(here, g.at[(*piece(f, i), pl.ds(256, 128))], target, sem["far", f, i])
 
     def gather_wait(name, g, f):
         sem = gathers[name]
-        wait_in(g.at[(*half(f, 1), pl.ds(128, 128))], sem["left", f, 1])
-        wait_in(g.at[(*half(f, 0), pl.ds(384, 128))], sem["right", f, 0])
-        for h in range(2):
-            wait_in(g.at[(*half(f, h), pl.ds(256, 128))], sem["far", f, h])
+        for i in pieces:
+            k, lanes = ("right", 384) if i < 2 else ("left", 128)
+            wait_in(g.at[(*piece(f, i), pl.ds(lanes, 128))], sem[k, f, i])
+            wait_in(g.at[(*piece(f, i), pl.ds(256, 128))], sem["far", f, i])
 
     w_sem = {}
 
     def weights_chan(l):
-        for p in range(1, 4):
-            w_sem["x", l, p] = pool.take()
-            their = (chan + p) % 4
-            send(
-                kern.at[l, :, pl.ds(their * 128 + core * 64 + y * 16, 16), :],
-                w.at[l, :, my_rows, pl.ds(128 * p, 128)],
-                at_chan(p), w_sem["x", l, p],
-            )
-
-    def weights_y(l):
-        load_w[l].wait()
-        for p in range(1, 4):
-            wait_in(w.at[l, :, my_rows, pl.ds(128 * p, 128)], w_sem["x", l, p])
-        for p in range(1, 4):
-            w_sem["y", l, p] = pool.take()
-            here = w.at[l, :, my_rows, :]
-            send(here, here, at_y(p), w_sem["y", l, p])
+        for i, (taps, index, _) in enumerate(w_parts):
+            for p in range(1, 4):
+                w_sem["x", l, i, p] = pool.take()
+                their = (chan + p) % 4
+                send(
+                    kern.at[l, taps, pl.ds(their * 128 + core * 64 + index * 16, 16), :],
+                    w.at[l, taps, w_rows(index), pl.ds(128 * p, 128)],
+                    at_chan(p), w_sem["x", l, i, p],
+                )
+
+    def weights_group(l):
+        for i, (taps, index, at_peer) in enumerate(w_parts):
+            load_w[l, i].wait()
+            for p in range(1, 4):
+                wait_in(w.at[l, taps, w_rows(index), pl.ds(128 * p, 128)], w_sem["x", l, i, p])
+            here = w.at[l, taps, w_rows(index), :]
+            for p in (2, 1, 3):
+                w_sem["group", l, i, p] = pool.take()
+                send(here, here, at_peer(p), w_sem["group", l, i, p])
 
     def weights_core(l):
-        for p in range(4):
-            if p:
-                wait_in(w.at[l, :, pl.ds(core * 64 + ((y + 4 - p) % 4) * 16, 16), :], w_sem["y", l, p])
-            w_sem["core", l, p] = pool.take()
-            here = w.at[l, :, pl.ds(core * 64 + ((y + 4 - p) % 4) * 16, 16), :]
-            send(here, here, sibling, w_sem["core", l, p])
+        for p in (0, 1, 3, 2):
+            for i, (taps, index, _) in enumerate(w_parts):
+                here = w.at[l, taps, w_rows((index + 4 - p) % 4), :]
+                if p:
+                    wait_in(here, w_sem["group", l, i, p])
+                w_sem["core", l, i, p] = pool.take()
+                send(here, here, sibling, w_sem["core", l, i, p])
 
     def weights_wait(l):
-        for p in range(4):
-            wait_in(w.at[l, :, pl.ds((1 - core) * 64 + ((y + 4 - p) % 4) * 16, 16), :], w_sem["core", l, p])
+        for p in (0, 1, 3, 2):
+            for i, (taps, index, _) in enumerate(w_parts):
+                wait_in(w.at[l, taps, w_rows((index + 4 - p) % 4, 1 - core), :], w_sem["core", l, i, p])
 
     rim_sem = {}
 
@@ -213,32 +248,40 @@
         pl.when(has_prev)(lambda: wait_in(pad.at[:, pl.ds(0, 128), :], up))
         pl.when(has_next)(lambda: wait_in(pad.at[:, pl.ds(128 + PX, 128), :], down))
 
-    def transpose_act(pad):
+    def transpose_act(l, pad, first, step, count):
         lane = lax.broadcasted_iota(jnp.int32, (128, 128), 1)
 
         def body(i, carry):
-            f, row = i // 10, i % 10
-            v = pad[f, pl.ds(row * 128, 128), :].astype(F32)
+            f, row = i // count, first + step * (i % count)
+            v = pad[f, pl.ds(pl.multiple_of(row * 128, 128), 128), :].astype(F32)
             a = (v * sigmoid(v)).astype(BF).astype(F32).T
             at = pl.ds(pl.multiple_of(row * 128, 128), 128)
             before = jnp.where(lane == 0, 0.0, pltpu.roll(a, 1, 1))
             after = jnp.where(lane == 127, 0.0, pltpu.roll(a, 127, 1))
-            actt[f, pl.ds(0, 128), at] = before.astype(BF)
-            actt[f, pl.ds(128, 128), at] = a.astype(BF)
-            actt[f, pl.ds(256, 128), at] = after.astype(BF)
+            actt[l, f, pl.ds(0, 128), at] = before.astype(BF)
+            actt[l, f, pl.ds(128, 128), at] = a.astype(BF)
+            actt[l, f, pl.ds(256, 128), at] = after.astype(BF)
             return carry
 
-        lax.fori_loop(0, 20, body, 0)
+        lax.fori_loop(0, 2 * count, body, 0)
+
+    def act_inner(l, pad):
+        transpose_act(l, pad, 1, 1, 8)
+
+    def act_rims(l, pad):
+        transpose_act(l, pad, 0, 9, 2)
 
     def kernel_grad(l, g, f):
         cotangent = g[f, inside, :]
         for r in range(3):
-            part = jnp.dot(actt[f, :, pl.ds(128 * r, PX)], cotangent, preferred_element_type=F32)
+            part = jnp.dot(actt[l, f, :, pl.ds(128 * r, PX)], cotangent, preferred_element_type=F32)
             for k in range(4):
                 block = part[:, 128 * k : 128 * k + 128].reshape(3, 128, 128)
                 if f:
                     block = block + red[l, k, pl.ds(3 * r, 3)]
                 red[l, k, pl.ds(3 * r, 3)] = block
+            if f:
+                reduce_core(l, r)
 
     def weight_rows(l, r):
         return w[l, pl.ds(3 * r, 3)].reshape(384, 512)
@@ -260,19 +303,27 @@
         send(halo_out.at[l, f, 0], halo_in.at[l, f, 1], prev, down, has_prev)
         send(halo_out.at[l, f, 1], halo_in.at[l, f, 0], nxt, up, has_next)
 
-    def back_rows(l, g, f):
+    def back_rows(l, g, f, i):
+        start = i * 256
+        acc = jnp.zeros((256, 384), F32)
+        for r in range(3):
+            rows = pl.ds(pl.multiple_of(start + (2 - r) * 128, 128), 256)
+            acc = acc + nt_dot(g[f, rows, :], weight_rows(l, r))
+        return join_taps(acc)
+
+    def back_inner(l, g, f):
         def body(i, carry):
-            start = i * 256
-            acc = jnp.zeros((256, 384), F32)
-            for r in range(3):
-                rows = pl.ds(pl.multiple_of(start + (2 - r) * 128, 128), 256)
-                acc = acc + nt_dot(g[f, rows, :], weight_rows(l, r))
-            back[pl.ds(pl.multiple_of(start, 128), 256), :] = join_taps(acc)
+            finish(l, f, i * 256, back_rows(l, g, f, i))
             return carry
 
-        lax.fori_loop(0, 4, body, 0)
-
-    def halos_add(l, f):
+        lax.fori_loop(1, 3, body, 0)
+
+    def back_outer(l, g, f):
+        def body(i, carry):
+            back[pl.ds(pl.multiple_of(i * 256, 256), 256), :] = back_rows(l, g, f, i * 3)
+            return carry
+
+        lax.fori_loop(0, 2, body, 0)
         up, down = halo_sem[l, f]
 
         @pl.when(has_prev)
@@ -283,38 +334,35 @@
         @pl.when(has_next)
         def _():
             wait_in(halo_in.at[l, f, 1], down)
-            back[pl.ds(PX - 128, 128), :] = back[pl.ds(PX - 128, 128), :] + halo_in[l, f, 1]
-
-    def middle_grad(f):
-        def body(i, carry):
-            rows = pl.ds(pl.multiple_of(i * 128, 128), 128)
-            padded = pl.ds(pl.multiple_of(i * 128 + 128, 128), 128)
+            back[pl.ds(384, 128), :] = back[pl.ds(384, 128), :] + halo_in[l, f, 1]
+
+        def close(i, carry):
+            finish(l, f, i * 768, back[pl.ds(pl.multiple_of(i * 256, 256), 256), :])
+            return carry
+
+        lax.fori_loop(0, 2, close, 0)
+
+    def finish(l, f, start, total):
+        rows = pl.ds(pl.multiple_of(start, 128), 256)
+        padded = pl.ds(pl.multiple_of(start + 128, 128), 256)
+        if l:
             v = midpad[f, padded, :].astype(F32)
-            gmg[f, padded, pl.ds(0, 128)] = (back[rows, :] * dsilu(v)).astype(BF)
-            return carry
-
-        lax.fori_loop(0, 8, body, 0)
-
-    def input_grad(f):
-        def body(i, carry):
-            rows = pl.ds(pl.multiple_of(i * 128, 128), 128)
-            padded = pl.ds(pl.multiple_of(i * 128 + 128, 128), 128)
+            gmg[f, padded, pl.ds(0, 128)] = (total * dsilu(v)).astype(BF)
+        else:
             v = xpad[f, padded, :].astype(F32)
             og = gog[f, padded, pl.ds(0, 128)].astype(F32)
-            ig_buf[f, rows, :] = (og + back[rows, :] * dsilu(v)).astype(BF)
-            return carry
-
-        lax.fori_loop(0, 8, body, 0)
+            ig_buf[f, rows, :] = (og + total * dsilu(v)).astype(BF)
 
     r_sem = {}
 
     def slot_of(block):
         return (chan + 4 - block) % 4
 
-    def reduce_core(l):
+    def reduce_core(l, r):
         for h in range(2):
-            r_sem["core", l, h] = pool.take()
-            send(red.at[l, slot_of(2 * h + 1 - core)], core_in.at[l, h], sibling, r_sem["core", l, h])
+            r_sem["core", l, h, r] = pool.take()
+            taps = pl.ds(3 * r, 3)
+            send(red.at[l, slot_of(2 * h + 1 - core), taps], core_in.at[l, h, taps], sibling, r_sem["core", l, h, r])
 
     def as_slab(v):
         return jnp.concatenate([v.reshape(72, 128), jnp.zeros((8, 128), F32)], axis=0).astype(BF)
@@ -322,8 +370,9 @@
     near_last = (2, 3, 1, 0)
 
     def reduce_y(l):
-        for h in range(2):
-            wait_in(core_in.at[l, h], r_sem["core", l, h])
+        for r in range(3):
+            for h in range(2):
+                wait_in(core_in.at[l, h, pl.ds(3 * r, 3)], r_sem["core", l, h, r])
         for p in (2, 1, 3, 0):
             q = (y + p) % 4
 
@@ -415,8 +464,11 @@
             ]
             rows = pl.ds(pl.multiple_of(dp_there * 128 + z_there * 32 + pair * 16, 16), 16)
             new_kern[l, :, rows, :] = jnp.concatenate(both, axis=1).astype(BF)
+        rows = pl.ds(pl.multiple_of(dp_there * 128 + z_there * 32, 32), 32)
+        pltpu.make_async_copy(new_kern.at[l, :, rows, :], kern_out.at[l, :, rows, :], sems.at[a_sem["store", l]]).start()
 
     def spread_core(l):
+        a_sem["store", l] = pool.take()
         for d in by_distance:
             dp_there, z_there = z_from(d)
             for p in range(1, 4):
@@ -433,79 +485,85 @@
             wait_in(slabs.at[l, dp_there, pl.ds(z_there * 4, 4)], a_sem["core", l, d])
             assemble(l, dp_there, z_there)
 
-    def og_half(f, h):
-        return og_in.at[f, pl.ds(512 * h, 512), :]
-
-    def mg_half(f, h):
-        return gmg.at[(*half(f, h), pl.ds(0, 128))]
+    def og_piece(f, i):
+        return og_in.at[f, pl.ds(256 * i, 256), :]
+
+    def mg_piece(f, i):
+        return gmg.at[(*piece(f, i), pl.ds(0, 128))]
 
     weights_chan(1)
-    gather_own("og", gog, og_half, 0)
+    gather_own("og", gog, og_piece, 0, pieces)
     rims("mid", mid_in, midpad)
-    weights_y(1)
-    gather_forward("og", gog, 0)
     weights_chan(0)
-    gather_own("og", gog, og_half, 1)
+    hear_half()
+    clear_edges()
     load_mid.wait()
+    act_inner(1, midpad)
+    weights_group(1)
+    hear_ring()
+    gather_forward("og", gog, 0, (0, 3, 1, 2))
+    gather_own("og", gog, og_piece, 1, pieces)
+    hear_sibling()
     rims_wait("mid", midpad)
-    transpose_act(midpad)
+    act_rims(1, midpad)
+    weights_group(0)
+    rims("x", x_in, xpad)
+    load_x.wait()
+    act_inner(0, xpad)
     gather_wait("og", gog, 0)
     load_og.wait()
+    weights_core(1)
+    hear_chan()
     kernel_grad(1, gog, 0)
-    gather_forward("og", gog, 1)
-    weights_core(1)
-    rims("x", x_in, xpad)
-    weights_y(0)
+    gather_forward("og", gog, 1, (0, 3, 1, 2))
     weights_wait(1)
     back_halos(1, gog, 0)
-    back_rows(1, gog, 0)
-    halos_add(1, 0)
-    middle_grad(0)
-    gather_own("mg", gmg, mg_half, 0)
+    back_inner(1, gog, 0)
+    gather_own("mg", gmg, mg_piece, 0, (1, 2))
+    back_outer(1, gog, 0)
+    gather_own("mg", gmg, mg_piece, 0, (0, 3))
     gather_wait("og", gog, 1)
     back_halos(1, gog, 1)
+    back_inner(1, gog, 1)
+    gather_forward("mg", gmg, 0, (1, 2))
+    gather_own("mg", gmg, mg_piece, 1, (1, 2))
+    back_outer(1, gog, 1)
+    gather_forward("mg", gmg, 0, (0, 3))
+    gather_own("mg", gmg, mg_piece, 1, (0, 3))
     kernel_grad(1, gog, 1)
-    reduce_core(1)
-    back_rows(1, gog, 1)
-    gather_forward("mg", gmg, 0)
-    halos_add(1, 1)
-    middle_grad(1)
-    gather_own("mg", gmg, mg_half, 1)
     reduce_y(1)
+    hear_all()
     weights_core(0)
-    load_x.wait()
     rims_wait("x", xpad)
-    transpose_act(xpad)
+    act_rims(0, xpad)
     weights_wait(0)
     gather_wait("mg", gmg, 0)
+    gather_forward("mg", gmg, 1, (1, 2))
     kernel_grad(0, gmg, 0)
-    gather_forward("mg", gmg, 1)
+    gather_forward("mg", gmg, 1, (0, 3))
     back_halos(0, gmg, 0)
-    back_rows(0, gmg, 0)
-    reduce_z(1)
-    halos_add(0, 0)
-    input_grad(0)
     gather_wait("mg", gmg, 1)
     kernel_grad(0, gmg, 1)
-    reduce_core(0)
+    reduce_z(1)
+    reduce_y(0)
     back_halos(0, gmg, 1)
-    reduce_y(0)
+    back_inner(0, gmg, 0)
+    back_outer(0, gmg, 0)
     adam(1)
-    back_rows(0, gmg, 1)
-    halos_add(0, 1)
-    input_grad(1)
+    reduce_z(0)
+    back_inner(0, gmg, 1)
+    back_outer(0, gmg, 1)
     stores = [load(ig_buf, ig_out)]
-    reduce_z(0)
     spread_y(1)
     adam(0)
     stores += [load(adam_out.at[k], ref) for k, ref in enumerate((master_out, moment_out, second_out))]
     spread_core(1)
     spread_y(0)
     spread_wait(1)
-    stores.append(load(new_kern.at[1], kern_out.at[1]))
     spread_core(0)
     spread_wait(0)
-    stores.append(load(new_kern.at[0], kern_out.at[0]))
+    for l in range(2):
+        wait_in(new_kern.at[l], a_sem["store", l])
     for copy in stores:
         copy.wait()
     for copy, when in sends:
@@ -555,9 +613,9 @@
             pltpu.VMEM((2, PX + 256, 512), BF),
             pltpu.VMEM((2, PX + 256, 512), BF),
             pltpu.VMEM((2, 9, 128, 512), BF),
-            pltpu.VMEM((2, 384, PX + 256), BF),
+            pltpu.VMEM((2, 2, 384, PX + 256), BF),
             pltpu.VMEM((2, 4, 9, 128, 128), F32),
-            pltpu.VMEM((PX, 128), F32),
+            pltpu.VMEM((512, 128), F32),
             pltpu.VMEM((2, 2, 2, 128, 128), F32),
             pltpu.VMEM((2, 2, 2, 128, 128), F32),
             pltpu.VMEM((2, 2, 9, 128, 128), F32),
@@ -571,6 +629,7 @@
             pltpu.VMEM((2, 9, 512, 128), BF),
             pltpu.VMEM((2, PX, 128), BF),
             pltpu.SemaphoreType.DMA((SEMS,)),
+            pltpu.SemaphoreType.REGULAR((4,)),
         ],
         compiler_params=pltpu.CompilerParams(
             collective_id=0, has_side_effects=True, vmem_limit_bytes=VMEM_LIMIT

time: 102 us -> 95.4 us (0.935)
  Pallas kernels: 101 us -> 94.5 us
    pallas_call x1, Pallas kernels: 98.3 us -> 91.6 us  [on_device(): pl.pallas_call(kernel, out_shape=results, in_specs=[any_space] * 7, out_s...]
where the time goes in v3:
time: 95.4 us; the launch traced here: 95.3 us
  Pallas kernels  94.5 us (99%)
    pallas_call x1, Pallas kernels, on_device(): pl.pallas_call(kernel, out_shape=results, in_specs=[any_space] * 7, out_s...  91.6 us
    pallas_call x1, Pallas kernels, on_device(): pl.pallas_call(hand_over, out_shape=results, in_specs=[any_space] * 5, ou...  2.87 us

profile of v3, /device:TPU:1, one launch (start us, length us, event | category | flops | bytes accessed | tf_op | source)
XLA Modules:
  0.0 95.3 jit_solution(13907451495533643842)
XLA Ops:
  0.6 91.6 %shard_map.110 = (bf16[2,1024,128]{2,1,0:T(8,128)(2,1)}, bf16[2,9,512,128]{3,2,1,0:T(8,128)(2,1)}, f32[2,9,8,128]{3,2,1,0:T(8,128)}, f32[2,9,8,128]{3,2,1,0:T(8,128)}, f32[2,9,8,128]{3,2,1,0:T(8,128)}) custom-call(bf16[2,1024,128]{2,1,0:T(8,128)(2,1)} %bitcast.14, bf16[2,1024,128]{2,1,0:T(8,128)(2,1)} %bitcast.15, bf16[2,1024,128]{2,1,0:T(8,128)(2,1)} %bitcast.16, ...), custom_call_target="tpu_custom_call" | custom-call | flops 10000000000 | bytes 10000000 | tf_op jit(solution)/shard_map/pallas_call | solution.py:605
  92.2 2.9 %shard_map.111 = (bf16[2,1024,128]{2,1,0:T(8,128)(2,1)}, bf16[2,9,512,128]{3,2,1,0:T(8,128)(2,1)}, f32[2,9,8,128]{3,2,1,0:T(8,128)}, f32[2,9,8,128]{3,2,1,0:T(8,128)}, f32[2,9,8,128]{3,2,1,0:T(8,128)}) custom-call(bf16[2,1024,128]{2,1,0:T(8,128)(2,1)} %get-tuple-element.15.ig, bf16[2,9,512,128]{3,2,1,0:T(8,128)(2,1)} %get-tuple-element.16.kern, ...), custom_call_target="tpu_custom_call" | custom-call | tf_op jit(solution)/shard_map/pallas_call | solution.py:642

commit v4 on v3

--- a/solution.py
+++ b/solution.py
@@ -368,15 +368,16 @@
         return jnp.concatenate([v.reshape(72, 128), jnp.zeros((8, 128), F32)], axis=0).astype(BF)
 
     near_last = (2, 3, 1, 0)
+    z_first = z_lo + 2 * ((chan // 2 + z_hi) % 2)
 
     def reduce_y(l):
         for r in range(3):
             for h in range(2):
                 wait_in(core_in.at[l, h, pl.ds(3 * r, 3)], r_sem["core", l, h, r])
-        for p in (2, 1, 3, 0):
-            q = (y + p) % 4
-
-            def body(c, carry, q=q):
+        for j in near_last:
+            c = (z_first + j) % 4
+
+            def body(q, carry, c=c):
                 rows = pl.ds(pl.multiple_of(c * 32 + q * 8, 8), 8)
                 for h in range(2):
                     total = red[l, slot_of(2 * h + core), :, rows, :] + core_in[l, h, :, rows, :]
@@ -384,15 +385,14 @@
                 return carry
 
             lax.fori_loop(0, 4, body, 0)
-            if p:
-                for j in near_last:
-                    r_sem["y", l, p, j] = pool.take()
-                    send(ysend.at[l, q, (z_lo + j) % 4], yrecv.at[l, p - 1, j], at_y(p), r_sem["y", l, p, j])
+            for p in (2, 1, 3):
+                r_sem["y", l, p, j] = pool.take()
+                send(ysend.at[l, (y + p) % 4, c], yrecv.at[l, p - 1, j], at_y(p), r_sem["y", l, p, j])
 
     def reduce_z(l):
         r_sem["z", l] = pool.take(8)
         for j in near_last:
-            c = (z_lo + j) % 4
+            c = (z_first + j) % 4
             for p in range(1, 4):
                 wait_in(yrecv.at[l, p - 1, j], r_sem["y", l, p, j])
             for h in range(2):
@@ -439,7 +439,6 @@
         for p in by_distance[1:]:
             a_sem["z", l, p] = pool.take()
             send(here, here, at_z(p), a_sem["z", l, p])
-        to_y(l, 0)
         adam_out[0, l] = new_master
         adam_out[1, l] = new_moment
         adam_out[2, l] = new_second
@@ -452,9 +451,10 @@
             send(here, here, at_y(p), a_sem["y", l, p, d])
 
     def spread_y(l):
-        for d in by_distance[1:]:
-            dp_there, z_there = z_from(d)
-            wait_in(slabs.at[l, dp_there, z_there * 4 + y], a_sem["z", l, d])
+        for d in by_distance:
+            if d:
+                dp_there, z_there = z_from(d)
+                wait_in(slabs.at[l, dp_there, z_there * 4 + y], a_sem["z", l, d])
             to_y(l, d)
 
     def assemble(l, dp_there, z_there):
@@ -525,12 +525,12 @@
     gather_wait("og", gog, 1)
     back_halos(1, gog, 1)
     back_inner(1, gog, 1)
+    kernel_grad(1, gog, 1)
     gather_forward("mg", gmg, 0, (1, 2))
     gather_own("mg", gmg, mg_piece, 1, (1, 2))
     back_outer(1, gog, 1)
     gather_forward("mg", gmg, 0, (0, 3))
     gather_own("mg", gmg, mg_piece, 1, (0, 3))
-    kernel_grad(1, gog, 1)
     reduce_y(1)
     hear_all()
     weights_core(0)
@@ -542,19 +542,19 @@
     kernel_grad(0, gmg, 0)
     gather_forward("mg", gmg, 1, (0, 3))
     back_halos(0, gmg, 0)
+    reduce_z(1)
     gather_wait("mg", gmg, 1)
     kernel_grad(0, gmg, 1)
-    reduce_z(1)
     reduce_y(0)
+    adam(1)
     back_halos(0, gmg, 1)
     back_inner(0, gmg, 0)
     back_outer(0, gmg, 0)
-    adam(1)
+    back_inner(0, gmg, 1)
     reduce_z(0)
-    back_inner(0, gmg, 1)
+    spread_y(1)
     back_outer(0, gmg, 1)
     stores = [load(ig_buf, ig_out)]
-    spread_y(1)
     adam(0)
     stores += [load(adam_out.at[k], ref) for k, ref in enumerate((master_out, moment_out, second_out))]
     spread_core(1)

time: 95.4 us -> 91.5 us (0.959)
  Pallas kernels: 94.5 us -> 90.6 us
    pallas_call x1, Pallas kernels: 91.6 us -> 87.7 us  [on_device(): pl.pallas_call(kernel, out_shape=results, in_specs=[any_space] * 7, out_s...]
where the time goes in v4:
time: 91.5 us; the launch traced here: 91.4 us
  Pallas kernels  90.6 us (99%)
    pallas_call x1, Pallas kernels, on_device(): pl.pallas_call(kernel, out_shape=results, in_specs=[any_space] * 7, out_s...  87.7 us
    pallas_call x1, Pallas kernels, on_device(): pl.pallas_call(hand_over, out_shape=results, in_specs=[any_space] * 5, ou...  2.87 us

profile of v4, /device:TPU:1, one launch (start us, length us, event | category | flops | bytes accessed | tf_op | source)
XLA Modules:
  0.0 91.4 jit_solution(1144529618041644670)
XLA Ops:
  0.6 87.7 %shard_map.110 = (bf16[2,1024,128]{2,1,0:T(8,128)(2,1)}, bf16[2,9,512,128]{3,2,1,0:T(8,128)(2,1)}, f32[2,9,8,128]{3,2,1,0:T(8,128)}, f32[2,9,8,128]{3,2,1,0:T(8,128)}, f32[2,9,8,128]{3,2,1,0:T(8,128)}) custom-call(bf16[2,1024,128]{2,1,0:T(8,128)(2,1)} %bitcast.14, bf16[2,1024,128]{2,1,0:T(8,128)(2,1)} %bitcast.15, bf16[2,1024,128]{2,1,0:T(8,128)(2,1)} %bitcast.16, ...), custom_call_target="tpu_custom_call" | custom-call | flops 10000000000 | bytes 10000000 | tf_op jit(solution)/shard_map/pallas_call | solution.py:605
  88.3 2.9 %shard_map.111 = (bf16[2,1024,128]{2,1,0:T(8,128)(2,1)}, bf16[2,9,512,128]{3,2,1,0:T(8,128)(2,1)}, f32[2,9,8,128]{3,2,1,0:T(8,128)}, f32[2,9,8,128]{3,2,1,0:T(8,128)}, f32[2,9,8,128]{3,2,1,0:T(8,128)}) custom-call(bf16[2,1024,128]{2,1,0:T(8,128)(2,1)} %get-tuple-element.15.ig, bf16[2,9,512,128]{3,2,1,0:T(8,128)(2,1)} %get-tuple-element.16.kern, ...), custom_call_target="tpu_custom_call" | custom-call | tf_op jit(solution)/shard_map/pallas_call | solution.py:642

commit v5 on v4

--- a/solution.py
+++ b/solution.py
@@ -525,9 +525,9 @@
     gather_wait("og", gog, 1)
     back_halos(1, gog, 1)
     back_inner(1, gog, 1)
-    kernel_grad(1, gog, 1)
     gather_forward("mg", gmg, 0, (1, 2))
     gather_own("mg", gmg, mg_piece, 1, (1, 2))
+    kernel_grad(1, gog, 1)
     back_outer(1, gog, 1)
     gather_forward("mg", gmg, 0, (0, 3))
     gather_own("mg", gmg, mg_piece, 1, (0, 3))
@@ -557,8 +557,8 @@
     stores = [load(ig_buf, ig_out)]
     adam(0)
     stores += [load(adam_out.at[k], ref) for k, ref in enumerate((master_out, moment_out, second_out))]
+    spread_y(0)
     spread_core(1)
-    spread_y(0)
     spread_wait(1)
     spread_core(0)
     spread_wait(0)

time: 91.5 us -> 91.4 us (level)
  no operation moved by 1% of the time
where the time goes in v5:
time: 91.4 us; the launch traced here: 91.3 us
  Pallas kernels  90.5 us (99%)
    pallas_call x1, Pallas kernels, on_device(): pl.pallas_call(kernel, out_shape=results, in_specs=[any_space] * 7, out_s...  87.6 us
    pallas_call x1, Pallas kernels, on_device(): pl.pallas_call(hand_over, out_shape=results, in_specs=[any_space] * 5, ou...  2.87 us

profile of v5, /device:TPU:1, one launch (start us, length us, event | category | flops | bytes accessed | tf_op | source)
XLA Modules:
  0.0 91.3 jit_solution(5818824005370466367)
XLA Ops:
  0.6 87.6 %shard_map.110 = (bf16[2,1024,128]{2,1,0:T(8,128)(2,1)}, bf16[2,9,512,128]{3,2,1,0:T(8,128)(2,1)}, f32[2,9,8,128]{3,2,1,0:T(8,128)}, f32[2,9,8,128]{3,2,1,0:T(8,128)}, f32[2,9,8,128]{3,2,1,0:T(8,128)}) custom-call(bf16[2,1024,128]{2,1,0:T(8,128)(2,1)} %bitcast.14, bf16[2,1024,128]{2,1,0:T(8,128)(2,1)} %bitcast.15, bf16[2,1024,128]{2,1,0:T(8,128)(2,1)} %bitcast.16, ...), custom_call_target="tpu_custom_call" | custom-call | flops 10000000000 | bytes 10000000 | tf_op jit(solution)/shard_map/pallas_call | solution.py:605
  88.3 2.9 %shard_map.111 = (bf16[2,1024,128]{2,1,0:T(8,128)(2,1)}, bf16[2,9,512,128]{3,2,1,0:T(8,128)(2,1)}, f32[2,9,8,128]{3,2,1,0:T(8,128)}, f32[2,9,8,128]{3,2,1,0:T(8,128)}, f32[2,9,8,128]{3,2,1,0:T(8,128)}) custom-call(bf16[2,1024,128]{2,1,0:T(8,128)(2,1)} %get-tuple-element.15.ig, bf16[2,9,512,128]{3,2,1,0:T(8,128)(2,1)} %get-tuple-element.16.kern, ...), custom_call_target="tpu_custom_call" | custom-call | tf_op jit(solution)/shard_map/pallas_call | solution.py:642

commit v6 on v5

--- a/solution.py
+++ b/solution.py
@@ -311,12 +311,12 @@
             acc = acc + nt_dot(g[f, rows, :], weight_rows(l, r))
         return join_taps(acc)
 
-    def back_inner(l, g, f):
+    def back_inner(l, g, f, first=1, end=3):
         def body(i, carry):
             finish(l, f, i * 256, back_rows(l, g, f, i))
             return carry
 
-        lax.fori_loop(1, 3, body, 0)
+        lax.fori_loop(first, end, body, 0)
 
     def back_outer(l, g, f):
         def body(i, carry):
@@ -518,8 +518,10 @@
     gather_forward("og", gog, 1, (0, 3, 1, 2))
     weights_wait(1)
     back_halos(1, gog, 0)
-    back_inner(1, gog, 0)
-    gather_own("mg", gmg, mg_piece, 0, (1, 2))
+    back_inner(1, gog, 0, 1, 2)
+    gather_own("mg", gmg, mg_piece, 0, (1,))
+    back_inner(1, gog, 0, 2, 3)
+    gather_own("mg", gmg, mg_piece, 0, (2,))
     back_outer(1, gog, 0)
     gather_own("mg", gmg, mg_piece, 0, (0, 3))
     gather_wait("og", gog, 1)

time: 91.4 us -> 92 us (level)
  no operation moved by 1% of the time
where the time goes in v6:
time: 92 us; the launch traced here: 91.9 us
  Pallas kernels  91.1 us (99%)
    pallas_call x1, Pallas kernels, on_device(): pl.pallas_call(kernel, out_shape=results, in_specs=[any_space] * 7, out_s...  88.2 us
    pallas_call x1, Pallas kernels, on_device(): pl.pallas_call(hand_over, out_shape=results, in_specs=[any_space] * 5, ou...  2.87 us

profile of v6, /device:TPU:1, one launch (start us, length us, event | category | flops | bytes accessed | tf_op | source)
XLA Modules:
  0.0 91.9 jit_solution(629993640846543834)
XLA Ops:
  0.6 88.2 %shard_map.110 = (bf16[2,1024,128]{2,1,0:T(8,128)(2,1)}, bf16[2,9,512,128]{3,2,1,0:T(8,128)(2,1)}, f32[2,9,8,128]{3,2,1,0:T(8,128)}, f32[2,9,8,128]{3,2,1,0:T(8,128)}, f32[2,9,8,128]{3,2,1,0:T(8,128)}) custom-call(bf16[2,1024,128]{2,1,0:T(8,128)(2,1)} %bitcast.14, bf16[2,1024,128]{2,1,0:T(8,128)(2,1)} %bitcast.15, bf16[2,1024,128]{2,1,0:T(8,128)(2,1)} %bitcast.16, ...), custom_call_target="tpu_custom_call" | custom-call | flops 10000000000 | bytes 10000000 | tf_op jit(solution)/shard_map/pallas_call | solution.py:607
  88.9 2.9 %shard_map.111 = (bf16[2,1024,128]{2,1,0:T(8,128)(2,1)}, bf16[2,9,512,128]{3,2,1,0:T(8,128)(2,1)}, f32[2,9,8,128]{3,2,1,0:T(8,128)}, f32[2,9,8,128]{3,2,1,0:T(8,128)}, f32[2,9,8,128]{3,2,1,0:T(8,128)}) custom-call(bf16[2,1024,128]{2,1,0:T(8,128)(2,1)} %get-tuple-element.15.ig, bf16[2,9,512,128]{3,2,1,0:T(8,128)(2,1)} %get-tuple-element.16.kern, ...), custom_call_target="tpu_custom_call" | custom-call | tf_op jit(solution)/shard_map/pallas_call | solution.py:644
